TPU v7x, 32 devices: a whole 2x2x4 slice. The times are simulated.
32 devices in a mesh: dp: 2 (over x), gx: 16 (over z, y, core).
Axes of the slice: x: 2, y: 2, z: 4, core: 2. Of those that a mesh axis runs over, the one named last changes fastest.
Arguments:
- field: bfloat16 [2, 16, 32, 128, 128], P('dp', 'gx'), may hold values from -6 to 6
- cotangent: bfloat16 [2, 16, 32, 128, 128], P('dp', 'gx'), may hold values from -6 to 6
- spectral_weight: bfloat16 [512, 16, 2048], P('gx'), may hold values from -3 to 3
- pointwise_weight: bfloat16 [32, 32], replicated, may hold values from -1 to 1
Outputs:
- field_grad: bfloat16 [2, 16, 32, 128, 128], P('dp', 'gx')
- weight_grad: float32 [512, 16, 2048], P('gx', 'dp')
All inputs are finite; a program needn't handle non-finite values.
Results may differ from a plain program's by a relative error of at most 0.001.
Values sent between devices are 32-bit elements; how exact they have to be, the bound alone decides.
No kernel may reach another device: no remote copies, remote signals or barrier semaphores. Data moves between devices by JAX's collectives and lax.ppermute only.
A program may use at most 64 MiB of HBM per device.

v0:
```python
import math

import jax
import jax.numpy as jnp
from jax import lax
from jax.sharding import PartitionSpec as P

M = 16


def kept_freqs(half_count, length):
    index_range = jnp.arange(2 * half_count, dtype=jnp.int32)
    return jnp.where(index_range < half_count, index_range, index_range + length - 2 * half_count)


def phase_tables(frequency, length):
    position = jnp.arange(length, dtype=jnp.int32)
    product = frequency[:, None] * position[None, :] % length
    angle_grid = product.astype(jnp.float32) * (2.0 * math.pi / length)
    return (jnp.cos(angle_grid), jnp.sin(angle_grid))


def rotation(cosine, sine):
    return jnp.stack([jnp.stack([cosine, -sine]), jnp.stack([sine, cosine])])


def einsum_exact(form, left, right):
    return jnp.einsum(form, left, right, precision=lax.Precision.HIGHEST)


def weight_terms(input_modes, cot_modes):
    in_real = input_modes[:, :, 0]
    in_imag = input_modes[:, :, 1]
    cot_real = cot_modes[:, :, 0]
    cot_imag = cot_modes[:, :, 1]
    grad_real = einsum_exact("skiq,skoq->qkio", in_real, cot_real) + einsum_exact(
        "skiq,skoq->qkio", in_imag, cot_imag
    )
    grad_imag = einsum_exact("skiq,skoq->qkio", in_real, cot_imag) - einsum_exact(
        "skiq,skoq->qkio", in_imag, cot_real
    )
    stacked = jnp.stack([grad_real, grad_imag], axis=2)
    return stacked.reshape(stacked.shape[0], stacked.shape[1], -1)


def on_device(field, cotangent, spectral_weight, pointwise_weight):
    planes = field.shape[1]
    channels = field.shape[2]
    length_y = field.shape[3]
    length_z = field.shape[4]
    width_x = planes * lax.axis_size("gx")
    kept_x = spectral_weight.shape[1]
    pair_local = spectral_weight.shape[0]
    cells_all = width_x * length_y * length_z
    cos_y, sin_y = phase_tables(kept_freqs(M, length_y), length_y)
    cos_z, sin_z = phase_tables(jnp.arange(M, dtype=jnp.int32), length_z)
    cos_x, sin_x = phase_tables(kept_freqs(kept_x // 2, width_x), width_x)
    forward_y = jnp.stack([cos_y, -sin_y])
    forward_z = rotation(cos_z.T, sin_z.T)
    forward_x = rotation(cos_x, sin_x)
    inverse_x = rotation(cos_x, -sin_x)
    inverse_y = rotation(cos_y, -sin_y)
    inverse_z = jnp.stack([cos_z, -sin_z])
    z_weight = jnp.where(jnp.arange(M) == 0, 1.0, 2.0).astype(jnp.float32) / cells_all
    weight_full = spectral_weight.astype(jnp.float32).reshape(
        pair_local, kept_x, 2, channels, channels
    )
    weight_real = weight_full[:, :, 0]
    weight_imag = weight_full[:, :, 1]

    def to_modes(data, mode_scale):
        values = data[0].astype(jnp.float32)
        along_y = einsum_exact("pcyz,rky->prckz", values, forward_y)
        mode_data = einsum_exact("prckz,rszm->psckm", along_y, forward_z * mode_scale)
        return mode_data.reshape(planes, 2, channels, -1)

    def along_x(plane_data):
        return einsum_exact("xrcq,rskx->kscq", plane_data, forward_x)

    input_local = to_modes(field, jnp.ones((M,), jnp.float32))
    cot_local = to_modes(cotangent, z_weight)
    input_planes, cot_planes = (
        lax.all_to_all(input_local, "gx", split_axis=3, concat_axis=0, tiled=True),
        lax.all_to_all(cot_local, "gx", split_axis=3, concat_axis=0, tiled=True),
    )
    input_modes = along_x(input_planes)
    cot_modes = along_x(cot_planes)
    cot_real = cot_modes[:, 0]
    cot_imag = cot_modes[:, 1]
    grad_real = einsum_exact("koq,qkio->kiq", cot_real, weight_real) + einsum_exact(
        "koq,qkio->kiq", cot_imag, weight_imag
    )
    grad_imag = einsum_exact("koq,qkio->kiq", cot_imag, weight_real) - einsum_exact(
        "koq,qkio->kiq", cot_real, weight_imag
    )
    grad_modes = jnp.stack([grad_real, grad_imag], axis=1)
    grad_planes = einsum_exact("krcq,rskx->xscq", grad_modes, inverse_x)
    returned = lax.all_to_all(grad_planes, "gx", split_axis=0, concat_axis=3, tiled=True)
    returned = returned.reshape(planes, 2, channels, 2 * M, M)
    along_y = einsum_exact("prckm,rsky->pscym", returned, inverse_y)
    spectral_part = einsum_exact("prcym,rmz->pcyz", along_y, inverse_z)
    linear_part = jnp.einsum(
        "pdyz,cd->pcyz", cotangent[0], pointwise_weight, preferred_element_type=jnp.float32
    )
    field_grad = (spectral_part + linear_part).astype(jnp.bfloat16)[None]
    local_terms = weight_terms(input_modes[None], cot_modes[None])
    weight_grad = lax.psum_scatter(local_terms, "dp", scatter_dimension=1, tiled=True)
    return (field_grad, weight_grad)


def solution(mesh):
    placed = (
        P("dp", "gx", None, None, None),
        P("dp", "gx", None, None, None),
        P("gx", None, None),
        P(),
    )
    return jax.shard_map(
        on_device,
        mesh=mesh,
        in_specs=placed,
        out_specs=(P("dp", "gx", None, None, None), P("gx", "dp", None)),
        check_vma=False,
    )
```

profile of v0, /device:TPU:0, one launch (start us, length us, event | category | flops | bytes accessed | tf_op | source)
XLA Modules:
  0.0 128.8 jit_solution(14275101296743397217)
XLA Ops:
  7.5 0.9 copy-done
  8.4 0.6 convolution_bitcast_fusion.1
  9.0 2.6 %convolution_bitcast_fusion.6 = f32[1,2,32,32,16]{3,4,2,1,0:T(8,128)S(1)} fusion(f32[2,32,32,128]{3,2,1,0:T(8,128)S(1)} %convolution_bitcast_fusion.1, f32[1,2,128,16]{2,3,0,1:T(8,128)S(1)} %get-tuple-element.25, f32[1,2,128,16]{2,3,0,1:T(8,128)S(1)} %get-tuple-element.24, f32[16]{0:T(128)S(1)} %fusion.72), kind=kOutput, calls=%fused_computation.22 | convolution fusion | flops 100679680 | bytes 1212480 | tf_op jit(solution)/shard_map/prckz,rszm->psckm/dot_general | solution.py:28
  11.5 0.4 copy.44
  11.9 0.4 copy.141
  12.3 1.2 reshape.527
  13.5 7.4 %all-to-all-start = ((f32[16,1,2048]{2,1,0:T(1,128)}), f32[16,1,2048]{2,1,0:T(1,128)S(1)}, u32[]{:S(2)}, u32[]{:S(2)}) async-start(f32[16,1,2048]{2,1,0:T(1,128)} %reshape.527), calls=%async_computation | async-start | bytes 262144 | tf_op jit(solution)/shard_map/all_to_all | solution.py:84
  20.9 1.8 %convolution_bitcast_fusion = f32[2,32,32,128]{3,2,1,0:T(8,128)S(1)} fusion(bf16[1,1,32,128,128]{4,3,2,1,0:T(8,128)(2,1)} %param.4, f32[1,32,128]{2,1,0:T(8,128)S(1)} %get-tuple-element.28, f32[1,32,128]{2,1,0:T(8,128)S(1)} %get-tuple-element.27), kind=kOutput, calls=%fused_computation.16 | convolution fusion | flops 402661376 | bytes 2129920 | tf_op jit(solution)/shard_map/pcyz,rky->prckz/dot_general | solution.py:28
  22.7 2.5 %convolution_bitcast_fusion.5 = f32[1,2,32,32,16]{3,4,2,1,0:T(8,128)S(1)} fusion(f32[2,32,32,128]{3,2,1,0:T(8,128)S(1)} %convolution_bitcast_fusion, f32[1,2,128,16]{2,3,0,1:T(8,128)S(1)} %get-tuple-element.25, f32[1,2,128,16]{2,3,0,1:T(8,128)S(1)} %get-tuple-element.24), kind=kOutput, calls=%fused_computation.21 | convolution fusion | flops 100671488 | bytes 1212416 | tf_op jit(solution)/shard_map/prckz,rszm->psckm/dot_general | solution.py:28
  25.3 0.4 copy.56
  25.6 0.4 copy.140
  26.1 1.2 reshape.531
  27.3 1.5 %all-to-all-done = f32[16,1,2048]{2,1,0:T(1,128)S(1)} async-done(((f32[16,1,2048]{2,1,0:T(1,128)}), f32[16,1,2048]{2,1,0:T(1,128)S(1)}, u32[]{:S(2)}, u32[]{:S(2)}) %all-to-all-start) | async-done | bytes 131104 | tf_op jit(solution)/shard_map/all_to_all | solution.py:84
  28.9 4.5 %all-to-all-start.2 = ((f32[16,1,2048]{2,1,0:T(1,128)}), f32[16,1,2048]{2,1,0:T(1,128)S(1)}, u32[]{:S(2)}, u32[]{:S(2)}) async-start(f32[16,1,2048]{2,1,0:T(1,128)} %reshape.531), calls=%async_computation.2 | async-start | bytes 262144 | tf_op jit(solution)/shard_map/all_to_all | solution.py:83
  33.4 0.5 broadcast.558
  34.0 0.9 reduce.8
  34.9 0.4 reshape.528
  35.3 0.5 copy.113
  35.8 0.6 fusion.17
  36.5 0.2 copy.60
  36.7 0.2 copy.62
  36.9 4.4 %all-to-all-done.2 = f32[16,1,2048]{2,1,0:T(1,128)S(1)} async-done(((f32[16,1,2048]{2,1,0:T(1,128)}), f32[16,1,2048]{2,1,0:T(1,128)S(1)}, u32[]{:S(2)}, u32[]{:S(2)}) %all-to-all-start.2) | async-done | bytes 131104 | tf_op jit(solution)/shard_map/all_to_all | solution.py:83
  41.3 0.9 reduce.10
  42.2 0.4 reshape.532
  42.7 0.5 copy.114
  43.1 0.6 convolution_bitcast_fusion.2
  43.8 0.2 copy.59
  44.0 0.2 copy.61
  44.2 4.8 %add_bitcast_fusion = (f32[32,16,1,32,32]{4,3,2,1,0:T(8,128)S(1)}, f32[32,16,1,32,32]{4,3,2,1,0:T(8,128)S(1)}) fusion(f32[32,16,32]{2,1,0:T(8,128)S(1)} %copy.62, f32[32,16,32]{2,1,0:T(8,128)S(1)} %copy.61, f32[32,16,32]{2,1,0:T(8,128)S(1)} %copy.60, f32[32,16,32]{2,1,0:T(8,128)S(1)} %copy.59), kind=kLoop, calls=%fused_computation.10 | loop fusion | flops 3145728 | bytes 4456448 | tf_op jit(solution)/shard_map/stack | solution.py:42
  49.0 7.3 %pad_maximum_fusion = f32[32,16,2,32,32]{4,3,2,1,0:T(8,128)} fusion(f32[32,16,1,32,32]{4,3,2,1,0:T(8,128)S(1)} %get-tuple-element.9, f32[32,16,1,32,32]{4,3,2,1,0:T(8,128)S(1)} %get-tuple-element.8), kind=kLoop, calls=%fused_computation | loop fusion | flops 1048576 | bytes 8388608 | tf_op jit(solution)/shard_map/stack | solution.py:42
  56.4 13.4 %reshape.495 = f32[32,16,2048]{2,1,0:T(8,128)} reshape(f32[32,16,2,32,32]{4,3,2,1,0:T(8,128)} %pad_maximum_fusion) | data formatting | bytes 8388608 | tf_op jit(solution)/shard_map/reshape | solution.py:43
  69.8 10.6 %reshape.485 = bf16[32,16,2,32,32]{4,3,2,1,0:T(8,128)(2,1)} reshape(bf16[32,16,2048]{2,1,0:T(8,128)(2,1)} %param.6) | data formatting | bytes 4194304 | tf_op jit(solution)/shard_map/reshape | solution.py:65
  80.5 0.2 copy.115
  80.7 0.2 copy.116
  80.9 11.3 %fusion.2 = (f32[16,32,32]{2,0,1:T(8,128)S(1)}, f32[16,32,32]{2,0,1:T(8,128)S(1)}, f32[16,32,32]{2,0,1:T(8,128)S(1)}, f32[16,32,32]{2,0,1:T(8,128)S(1)}) fusion(f32[16,32,32]{2,0,1:T(8,128)S(1)} %copy.116, bf16[32,16,2,32,32]{4,3,2,1,0:T(8,128)(2,1)} %reshape.485, f32[16,32,32]{2,0,1:T(8,128)S(1)} %copy.115), kind=kLoop, calls=%fused_computation.7 | loop fusion | flops 5177344 | bytes 2490368
  92.3 0.2 copy.76
  93.1 0.6 convolution_bitcast_fusion.4
  93.9 0.9 reshape.529
  94.9 3.7 %all-to-all-start.1 = ((f32[16,1,2048]{2,1,0:T(1,128)}), f32[16,1,2048]{2,1,0:T(1,128)S(1)}, u32[]{:S(2)}, u32[]{:S(2)}) async-start(f32[16,1,2048]{2,1,0:T(1,128)} %reshape.529), calls=%async_computation.1 | async-start | bytes 262144 | tf_op jit(solution)/shard_map/all_to_all | solution.py:98
  98.6 0.7 fusion.11
  99.3 6.9 %all-to-all-done.1 = f32[16,1,2048]{2,1,0:T(1,128)S(1)} async-done(((f32[16,1,2048]{2,1,0:T(1,128)}), f32[16,1,2048]{2,1,0:T(1,128)S(1)}, u32[]{:S(2)}, u32[]{:S(2)}) %all-to-all-start.1) | async-done | bytes 131104 | tf_op jit(solution)/shard_map/all_to_all | solution.py:98
  106.3 0.9 reduce.9
  107.2 1.0 reshape.530
  108.2 2.0 %copy.49 = f32[16,2,32,32]{2,3,0,1:T(8,128)} copy(f32[16,2,32,32]{3,2,1,0:T(8,128)} %reshape.530) | data formatting | bytes 262144 | tf_op jit(solution)/shard_map/all_to_all | solution.py:98
  110.2 2.1 %copy.51 = f32[2,32,32,16]{2,1,0,3:T(8,128)} copy(f32[2,32,32,16]{1,3,2,0:T(8,128)} %bitcast.241) | data formatting | bytes 262144 | tf_op jit(solution)/shard_map/reshape.10
  112.3 1.7 %convolution_bitcast_fusion.3 = f32[2,32,128,16]{2,1,3,0:T(8,128)S(1)} fusion(f32[2,32,32,16]{2,1,0,3:T(8,128)} %copy.51, f32[1,2,32,128]{3,2,1,0:T(8,128)S(1)} %get-tuple-element.17, f32[1,2,32,128]{3,2,1,0:T(8,128)S(1)} %get-tuple-element.16), kind=kOutput, calls=%fused_computation.19 | convolution fusion | flops 100679680 | bytes 720896 | tf_op jit(solution)/shard_map/prckm,rsky->pscym/dot_general | solution.py:28
  113.9 5.8 %fusion.5 = bf16[1,1,32,128,128]{4,3,2,1,0:T(8,128)(2,1)} fusion(f32[32,128,128]{2,0,1:T(8,128)S(1)} %fusion.11, f32[2,32,128,16]{2,1,3,0:T(8,128)S(1)} %convolution_bitcast_fusion.3, f32[1,16,128]{2,1,0:T(8,128)S(1)} %get-tuple-element.33, f32[1,16,128]{2,1,0:T(8,128)S(1)} %get-tuple-element.34), kind=kOutput, calls=%fused_computation.15 | convolution fusion | flops 202379264 | bytes 3686400 | tf_op jit(solution)/shard_map/prcym,rmz->pcyz/dot_general | solution.py:28
  119.7 2.2 %reduce-scatter.2.cloned.1.call-done = f32[32,8,2048]{2,1,0:T(8,128)} async-done(((f32[32,16,2048]{2,1,0:T(8,128)}), f32[32,8,2048]{2,1,0:T(8,128)}) %reduce-scatter.2.cloned.1.call-update) | async-done | bytes 2097168 | tf_op jit(solution)/shard_map/reduce_scatter | solution.py:107
  (25 shorter events, 1.5 us)
Async XLA Ops:
  7.2 1.2 copy-start
  13.5 15.3 %all-to-all-start = ((f32[16,1,2048]{2,1,0:T(1,128)}), f32[16,1,2048]{2,1,0:T(1,128)S(1)}, u32[]{:S(2)}, u32[]{:S(2)}) async-start(f32[16,1,2048]{2,1,0:T(1,128)} %reshape.527), calls=%async_computation | async-start | bytes 262144 | tf_op jit(solution)/shard_map/all_to_all | solution.py:84
  28.9 12.4 %all-to-all-start.2 = ((f32[16,1,2048]{2,1,0:T(1,128)}), f32[16,1,2048]{2,1,0:T(1,128)S(1)}, u32[]{:S(2)}, u32[]{:S(2)}) async-start(f32[16,1,2048]{2,1,0:T(1,128)} %reshape.531), calls=%async_computation.2 | async-start | bytes 262144 | tf_op jit(solution)/shard_map/all_to_all | solution.py:83
  33.4 88.5 %reduce-scatter.2.cloned.1.call-start = ((), (), s32[]{:S(2)}) async-start(), calls=%async_computation.4 | async-start | bytes 6291456 | tf_op jit(solution)/shard_map/reduce_scatter | solution.py:107
  80.9 17.7 %copy-start.1 = (bf16[32,32]{1,0:T(8,128)(2,1)S(1)}, bf16[32,32]{1,0:T(8,128)(2,1)}, u32[]{:S(2)}) copy-start(bf16[32,32]{1,0:T(8,128)(2,1)} %param.7) | copy-start | bytes 6148
  94.9 11.4 %all-to-all-start.1 = ((f32[16,1,2048]{2,1,0:T(1,128)}), f32[16,1,2048]{2,1,0:T(1,128)S(1)}, u32[]{:S(2)}, u32[]{:S(2)}) async-start(f32[16,1,2048]{2,1,0:T(1,128)} %reshape.529), calls=%async_computation.1 | async-start | bytes 262144 | tf_op jit(solution)/shard_map/all_to_all | solution.py:98
Sparse Core Ops, SparseCore 0:
  69.9 51.9 reduce-scatter.1
where the time goes:
time: 130 us; the launch traced here: 129 us
  local copies, waits for them, and re-layouts  39.4 us (30%)
  other arithmetic  26.8 us (21%)
  matrix products  17.4 us (13%)
  starting transfers between devices  15.7 us (12%)
  waiting for transfers between devices  15.1 us (12%)
  between operations  14.4 us (11%)
    dot_general x9, matrix products, einsum_exact(): return jnp.einsum(form, left, right, precision=lax.Precision.HIGHEST)  16.7 us
    reshape x1, local copies, waits for them, and re-layouts, weight_terms(): return stacked.reshape(stacked.shape[0], stacked.shape[1], -1)  13.4 us
    another operation x2, other arithmetic, weight_terms(): stacked = jnp.stack([grad_real, grad_imag], axis=2)  12.1 us
    unnamed x1, other arithmetic  11.3 us
    reshape x1, local copies, waits for them, and re-layouts, on_device(): spectral_weight.astype(jnp.float32)  10.6 us
    all_to_all x1, starting transfers between devices, on_device(): lax.all_to_all(cot_local, 'gx', split_axis=3, concat_axis=0, tiled=True)  7.4 us
    all_to_all x1, waiting for transfers between devices, on_device(): lax.all_to_all(grad_planes, 'gx', split_axis=0, concat_axis=3, tiled=True)  6.94 us
    unnamed x13, local copies, waits for them, and re-layouts  6.5 us
  transfers between devices with their start and end apart: 4, of which 4 were waited for; matrix products, arithmetic and copies ran while one was open for 38% of the time, Pallas kernels for 0%

commit v1 on v0

v1 whole, which is shorter than its diff:
```python
import math

import jax
import jax.numpy as jnp
import ml_dtypes
import numpy as np
from jax import lax
from jax.experimental import pallas as pl
from jax.experimental.pallas import tpu as pltpu
from jax.sharding import PartitionSpec as P

M = 16
F32 = jnp.float32
BF16 = jnp.bfloat16
VMEM_LIMIT = 56 * 1024 * 1024


def kept_freqs(half_count, length):
    index = np.arange(2 * half_count)
    return np.where(index < half_count, index, index + length - 2 * half_count)


def phases(frequency, length):
    product = np.outer(frequency, np.arange(length)) % length
    angle = product * (2.0 * math.pi / length)
    return np.cos(angle), np.sin(angle)


def split_np(table):
    high = table.astype(ml_dtypes.bfloat16)
    low = (table - high.astype(np.float64)).astype(ml_dtypes.bfloat16)
    return high, low


def split(value):
    high = value.astype(BF16)
    low = (value - high.astype(F32)).astype(BF16)
    return high, low


def dot(left, right):
    return jnp.dot(left, right, preferred_element_type=F32)


def forward_tables(length_y, length_z):
    cos_y, sin_y = phases(kept_freqs(M, length_y), length_y)
    high, low = split_np(np.concatenate([cos_y, -sin_y], 0))
    along_y = np.concatenate([high, low], 0)
    cos_z, sin_z = phases(np.arange(M), length_z)
    block = np.zeros((2, length_z, 2, M))
    block[0, :, 0], block[1, :, 0] = cos_z.T, sin_z.T
    block[0, :, 1], block[1, :, 1] = -sin_z.T, cos_z.T
    along_z = np.zeros((8, 2, length_z, 2, 8, M))
    for place in range(8):
        along_z[place, :, :, :, place, :] = block
    along_z = along_z.reshape(8, 2 * length_z, 2 * 8 * M)
    return along_y, np.stack(split_np(along_z))


def inverse_tables(length_y, length_z):
    cos_z, sin_z = phases(np.arange(M), length_z)
    along_z = np.zeros((2, 8, M, 8, 2, length_z))
    for place in range(8):
        along_z[0, place, :, place, 0] = cos_z
        along_z[1, place, :, place, 0] = -sin_z
        along_z[0, place, :, place, 1] = sin_z
        along_z[1, place, :, place, 1] = cos_z
    along_z = along_z.reshape(2 * 8 * M, 8 * 2 * length_z)
    cos_y, sin_y = phases(kept_freqs(M, length_y), length_y)
    high, low = split_np(np.concatenate([cos_y.T, -sin_y.T], 1))
    return np.stack(split_np(along_z)), np.concatenate([high, high, low], 1)


def x_tables(kept_x, width_x):
    cos_x, sin_x = phases(kept_freqs(kept_x // 2, width_x), width_x)
    high, low = split_np(np.concatenate([cos_x, sin_x], 1))
    forward = np.concatenate([high, high, low], 1)
    high, low = split_np(np.concatenate([cos_x.T, sin_x.T], 1))
    inverse = np.concatenate([high, high, low], 1)
    return forward, inverse


def spread_table(channels):
    copies = 128 // channels
    table = np.zeros((2, 2, 2, channels, 2, copies, channels))
    eye = np.eye(channels)
    for part in range(2):
        table[:, part, 1, :, part] = eye[:, None, :]
    return table.reshape(8 * channels, 256).astype(ml_dtypes.bfloat16)


def gather_table(channels):
    table = np.zeros((2, channels, channels, 2, 2, 2, channels))
    for i in range(channels):
        table[0, i, :, 0, :, 0, i] = 1.0
        table[1, i, :, 0, :, 1, i] = 1.0
        table[1, i, :, 1, :, 0, i] = -1.0
        table[0, i, :, 1, :, 1, i] = 1.0
    return table.reshape(2 * channels * channels, 8 * channels).astype(ml_dtypes.bfloat16)


def repeat_table(channels):
    square = channels * channels
    table = np.zeros((2, 2, 2, channels, 2 * square + 256))
    for i in range(channels):
        for part in range(2):
            start = part * square + i * channels
            table[:, part, 0, i, start : start + channels] = 1.0
            table[:, part, 1, i, 2 * square + part * 128 + i : 2 * square + part * 128 + 128 : channels] = 1.0
    return table.reshape(8 * channels, -1).astype(ml_dtypes.bfloat16)


def forward_kernel(scale_ref, field_ref, cot_ref, fy_ref, fz_ref, out_ref, rows_ref):
    channels, length_y, length_z = field_ref.shape
    kept = 4 * M
    for array, ref in enumerate((field_ref, cot_ref)):
        for pair in range(channels // 2):
            data = jnp.concatenate([ref[2 * pair], ref[2 * pair + 1]], axis=1)
            both = dot(fy_ref[...], data)
            value = both[:kept] + both[kept:]
            start = (array * channels + 2 * pair) * kept
            rows_ref[start : start + kept, :] = value[:, :length_z]
            rows_ref[start + kept : start + 2 * kept, :] = value[:, length_z:]
    count = 2 * channels
    total = None
    for place in range(8):
        pieces = []
        for group in range(2 * M // 8):
            ky = group * 8 + place
            real = rows_ref[pl.ds(ky, count, stride=kept), :]
            imag = rows_ref[pl.ds(2 * M + ky, count, stride=kept), :]
            pieces.append(jnp.concatenate([real, imag], axis=1))
        high, low = split(jnp.concatenate(pieces, axis=0))
        size = high.shape[0]
        both = dot(jnp.concatenate([high, low], axis=0), fz_ref[0, place])
        term = both[:size] + both[size:] + dot(high, fz_ref[1, place])
        total = term if total is None else total + term
    for group in range(2 * M // 8):
        block = total[group * count : (group + 1) * count] * scale_ref[...]
        stacked = jnp.concatenate([block[:, :128], block[:, 128:]], axis=0)
        out_ref[group * 128 : (group + 1) * 128, :] = stacked.T


def mid_kernel(
    planes_ref, weight_ref, fx_ref, ix_ref, spread_ref, gather_ref,
    modes_ref, out_ref, rows_ref, high_ref, low_ref,
):
    pairs, kept_x, _ = weight_ref.shape
    width_x = planes_ref.shape[0] // pairs
    pack = width_x * pairs // out_ref.shape[0]
    halves, _, share, lanes = modes_ref.shape
    lane = lax.broadcasted_iota(jnp.int32, (width_x, 128), 1)
    sign = jnp.where(lane < 64, 1.0, -1.0).astype(F32)
    for step in range(pairs // 2):
        columns = []
        for q in (2 * step, 2 * step + 1):
            plane = planes_ref[pl.ds(q, width_x, stride=pairs), :]
            turned = pltpu.roll(plane, 64, 1) * sign
            columns.append(jnp.concatenate([plane, turned], axis=0))
        high, low = split(jnp.concatenate(columns, axis=1))
        modes = dot(fx_ref[...], jnp.concatenate([high, low, high], axis=0))
        for index, q in enumerate((2 * step, 2 * step + 1)):
            mode = modes[:, index * 128 : (index + 1) * 128]
            rows_ref[q * kept_x : (q + 1) * kept_x, :] = mode
            for half in range(halves):
                modes_ref[half, q] = mode[half * share : (half + 1) * share]
    square = weight_ref.shape[2] // 2
    for q in range(pairs):
        high, low = split(rows_ref[q * kept_x : (q + 1) * kept_x, :])
        spread = dot(jnp.concatenate([high, low], axis=1), spread_ref[...])
        real, imag = spread[:, :128], spread[:, 128:]
        rows = pl.ds(q * kept_x, kept_x)
        for start in range(0, square, 128):
            w_real = weight_ref[q, :, start : start + 128].astype(F32)
            w_imag = weight_ref[q, :, square + start : square + start + 128].astype(F32)
            first = split(real * w_real + imag * w_imag)
            second = split(imag * w_real - real * w_imag)
            high_ref[rows, start : start + 128] = first[0]
            low_ref[rows, start : start + 128] = first[1]
            high_ref[rows, square + start : square + start + 128] = second[0]
            low_ref[rows, square + start : square + start + 128] = second[1]
    grads = dot(high_ref[...], gather_ref[...]) + dot(low_ref[...], gather_ref[...])
    count = pairs // pack
    if pack == 2:
        size = count * kept_x
        lane = lax.broadcasted_iota(jnp.int32, (size, 256), 1) % 128
        grads = jnp.where(lane < 64, grads[:size], grads[size:])
    for step in range(count // 2):
        columns = []
        for row in (2 * step, 2 * step + 1):
            block = grads[row * kept_x : (row + 1) * kept_x]
            columns.append(jnp.concatenate([block[:, :128], block[:, 128:]], axis=0))
        high, low = split(jnp.concatenate(columns, axis=1))
        planes = dot(ix_ref[...], jnp.concatenate([high, low, high], axis=0))
        for index, row in enumerate((2 * step, 2 * step + 1)):
            out_ref[pl.ds(row, width_x, stride=count), :] = planes[:, index * 128 : (index + 1) * 128]


def weight_kernel(mine_ref, other_ref, repeat_ref, out_ref):
    pairs, share, _ = mine_ref.shape
    square = out_ref.shape[2] // 2
    chunk = min(pairs, 8)

    @pl.loop(0, pairs // chunk)
    def _(step):
        base = step * chunk
        sides = []
        for ref in (mine_ref, other_ref):
            rows = ref[pl.ds(base, chunk)].reshape(chunk * share, 128)
            high, low = split(rows)
            sides.append(jnp.concatenate([high, low], axis=1))
        spread = [dot(side, repeat_ref[:, 2 * square :]) for side in sides]
        for start in range(0, square, 256):
            real = imag = None
            for side, cots in zip(sides, spread):
                f_real = dot(side, repeat_ref[:, start : start + 256])
                f_imag = dot(side, repeat_ref[:, square + start : square + start + 256])
                c_real = jnp.concatenate([cots[:, :128]] * 2, axis=1)
                c_imag = jnp.concatenate([cots[:, 128:]] * 2, axis=1)
                one = f_real * c_real + f_imag * c_imag
                two = f_real * c_imag - f_imag * c_real
                real = one if real is None else real + one
                imag = two if imag is None else imag + two
            out_ref[pl.ds(base, chunk), :, start : start + 256] = real.reshape(chunk, share, 256)
            out_ref[pl.ds(base, chunk), :, square + start : square + start + 256] = imag.reshape(
                chunk, share, 256
            )


def inverse_kernel(planes_ref, cot_ref, mix_ref, iz_ref, iy_ref, out_ref, rows_ref, linear_ref):
    channels, length_y, length_z = cot_ref.shape
    rows, _ = planes_ref.shape
    pack = 2 * M * M // rows
    kept = 4 * M
    pieces = []
    order = []
    for block in range(rows // 128):
        turned = planes_ref[block * 128 : (block + 1) * 128, :].T
        for low_bit in range(pack):
            start = low_bit * 2 * channels
            pieces.append(
                jnp.concatenate(
                    [turned[start : start + channels], turned[start + channels : start + 2 * channels]], axis=1
                )
            )
            order.append((block, low_bit))
    high, low = split(jnp.concatenate(pieces, axis=0))
    size = high.shape[0]
    both_terms = jnp.concatenate([high, low], axis=0)
    for place in range(8):
        for part in range(2):
            column = (place * 2 + part) * length_z
            both = dot(both_terms, iz_ref[0, :, column : column + length_z])
            value = both[:size] + both[size:] + dot(high, iz_ref[1, :, column : column + length_z])
            for index, (block, low_bit) in enumerate(order):
                ky = (block * 8 + place) * pack + low_bit
                start = (part * 2 * M + ky) * channels
                rows_ref[start : start + channels, :] = value[index * channels : (index + 1) * channels]
    for step in range(length_y // 32):
        columns = []
        for part in range(2):
            first = step * 32 + part * 16
            columns.append(cot_ref[:, first : first + 16, :].reshape(channels * 16, length_z))
        mixed = dot(mix_ref[...], jnp.concatenate(columns, axis=1))
        for part in range(2):
            first = step * 32 + part * 16
            linear_ref[:, first : first + 16, :] = mixed[:, part * length_z : (part + 1) * length_z].reshape(
                channels, 16, length_z
            )
    for pair in range(channels // 2):
        columns = [rows_ref[pl.ds(2 * pair + side, kept, stride=channels), :] for side in range(2)]
        high, low = split(jnp.concatenate(columns, axis=1))
        value = dot(iy_ref[...], jnp.concatenate([high, low, high], axis=0))
        for side in range(2):
            channel = 2 * pair + side
            spectral = value[:, side * length_z : (side + 1) * length_z]
            out_ref[channel] = (spectral + linear_ref[channel]).astype(BF16)


def call(kernel, out_shape, scratch, flops, moved, *args):
    return pl.pallas_call(
        kernel,
        out_shape=out_shape,
        scratch_shapes=scratch,
        compiler_params=pltpu.CompilerParams(vmem_limit_bytes=VMEM_LIMIT),
        cost_estimate=pl.CostEstimate(flops=flops, bytes_accessed=moved, transcendentals=0),
    )(*args)


def weight_terms(modes, channels):
    parts = modes.reshape(modes.shape[:3] + (2, 2, channels))
    in_real, in_imag = parts[..., 0, 0, :, None], parts[..., 1, 0, :, None]
    cot_real, cot_imag = parts[..., 0, 1, None, :], parts[..., 1, 1, None, :]
    real = jnp.sum(in_real * cot_real + in_imag * cot_imag, axis=0)
    imag = jnp.sum(in_real * cot_imag - in_imag * cot_real, axis=0)
    stacked = jnp.stack([real, imag], axis=2)
    return stacked.reshape(stacked.shape[:2] + (-1,))


def on_device(field, cotangent, spectral_weight, pointwise_weight):
    _, planes, channels, length_y, length_z = field.shape
    pairs, kept_x, _ = spectral_weight.shape
    groups = lax.axis_size("gx")
    samples = lax.axis_size("dp")
    width_x = planes * groups
    share = kept_x // samples
    pack = 2 if pairs == 2 * M else 1
    count = pairs // pack
    all_pairs = 2 * M * M
    cells = width_x * length_y * length_z
    shape = jax.ShapeDtypeStruct
    field = field.reshape(channels, length_y, length_z)
    cotangent = cotangent.reshape(channels, length_y, length_z)

    fy, fz = forward_tables(length_y, length_z)
    iz, iy = inverse_tables(length_y, length_z)
    fx, ix = x_tables(kept_x, width_x)
    scale = np.ones((2, channels, 2, 8, M), np.float32)
    scale[1] = np.where(np.arange(M) == 0, 1.0, 2.0) / cells
    scale = scale.reshape(2 * channels, 256)

    spectra = call(
        forward_kernel,
        shape((all_pairs, 128), F32),
        [pltpu.VMEM((2 * channels * 4 * M, length_z), F32)],
        10**9, 5 * 10**6,
        scale, field, cotangent, fy, fz,
    )
    received = lax.all_to_all(
        spectra.reshape(groups, pairs, 128), "gx", split_axis=0, concat_axis=0, tiled=True
    )
    modes, grads = call(
        mid_kernel,
        (shape((samples, pairs, share, 128), F32), shape((width_x * count, 128), F32)),
        [
            pltpu.VMEM((pairs * kept_x, 128), F32),
            pltpu.VMEM((pairs * kept_x, 2 * channels * channels), BF16),
            pltpu.VMEM((pairs * kept_x, 2 * channels * channels), BF16),
        ],
        10**9, 4 * 10**6,
        received.reshape(width_x * pairs, 128), spectral_weight, fx, ix,
        spread_table(channels), gather_table(channels),
    )
    returned = lax.all_to_all(
        grads.reshape(groups, count, 128), "gx", split_axis=0, concat_axis=0, tiled=True
    )
    if samples == 2 and share % 8 == 0:
        me = lax.axis_index("dp")
        mine = lax.dynamic_index_in_dim(modes, me, 0, keepdims=False)
        other = lax.dynamic_index_in_dim(modes, 1 - me, 0, keepdims=False)
        other = lax.ppermute(other, "dp", [(0, 1), (1, 0)])
        weight_grad = call(
            weight_kernel,
            shape((pairs, share, 2 * channels * channels), F32),
            [],
            10**9, 3 * 10**6,
            mine, other, repeat_table(channels),
        )
    else:
        modes = lax.all_to_all(modes, "dp", split_axis=0, concat_axis=0, tiled=True)
        weight_grad = weight_terms(modes, channels)

    eye = jnp.eye(16, dtype=BF16)
    mix = (pointwise_weight[:, None, :, None] * eye[None, :, None, :]).reshape(16 * channels, 16 * channels)
    field_grad = call(
        inverse_kernel,
        shape((channels, length_y, length_z), BF16),
        [pltpu.VMEM((4 * M * channels, length_z), F32), pltpu.VMEM((channels, length_y, length_z), F32)],
        10**9, 4 * 10**6,
        returned.reshape(width_x * count, 128), cotangent, mix, iz, iy,
    )
    return field_grad.reshape(1, planes, channels, length_y, length_z), weight_grad


def solution(mesh):
    placed = (
        P("dp", "gx", None, None, None),
        P("dp", "gx", None, None, None),
        P("gx", None, None),
        P(),
    )
    return jax.shard_map(
        on_device,
        mesh=mesh,
        in_specs=placed,
        out_specs=(P("dp", "gx", None, None, None), P("gx", "dp", None)),
        check_vma=False,
    )
```

time: 130 us -> 59.1 us (0.45)
  local copies, waits for them, and re-layouts: 39.4 us -> 12.1 us
  other arithmetic: 26.8 us -> 2.3 us
  Pallas kernels: 0 us -> 21.3 us
  matrix products: 17.4 us -> 0 us
  between operations: 14.4 us -> 0.67 us
  waiting for transfers between devices: 15.1 us -> 10 us
  starting transfers between devices: 15.7 us -> 12.4 us
    reshape x4 -> x0, local copies, waits for them, and re-layouts: 24.8 us -> none  [the longest x1 13.4 us: weight_terms(): return stacked.reshape(stacked.shape[0], stacked.shape[1], -1)]
    pallas_call x0 -> x4, Pallas kernels: none -> 21.3 us  [call(): pl.pallas_call(kernel, out_shape=out_shape, scratch_shapes=scratch, compi...]
    dot_general x10 -> x0, matrix products: 17.4 us -> none  [the longest x9 16.7 us: einsum_exact(): return jnp.einsum(form, left, right, precision=lax.Precision.HIGHEST)]
    another operation x7 -> x0, other arithmetic: 12.2 us -> none  [the longest x2 12.1 us: weight_terms(): stacked = jnp.stack([grad_real, grad_imag], axis=2)]
    unnamed x1 -> x0, other arithmetic: 11.3 us -> none
    mul x0 -> x1, local copies, waits for them, and re-layouts: none -> 8.41 us  [on_device(): pointwise_weight[:, None, :, None] * eye[None, :, None, :]]
    all_to_all x3 -> x2, starting transfers between devices: 15.6 us -> 10.9 us  [the longest x1 7.38 us: on_device(): lax.all_to_all(spectra.reshape(groups, pairs, 128), 'gx', split_axis=0, c...]
    unnamed x13 -> x8, local copies, waits for them, and re-layouts: 6.5 us -> 1.99 us
  transfers between devices with their start and end apart: 4 -> 3, of which waited for: 4 -> 1; matrix products, arithmetic and copies ran while one was open for 38% -> 21% of each run, Pallas kernels for 0% -> 8%
where the time goes in v1:
time: 59.1 us; the launch traced here: 58.7 us
  Pallas kernels  21.3 us (36%)
  starting transfers between devices  12.4 us (21%)
  local copies, waits for them, and re-layouts  12.1 us (20%)
  waiting for transfers between devices  10 us (17%)
  other arithmetic  2.3 us (4%)
  between operations  0.67 us (1%)
    pallas_call x4, Pallas kernels, call(): pl.pallas_call(kernel, out_shape=out_shape, scratch_shapes=scratch, compi...  21.3 us
    all_to_all x1, waiting for transfers between devices, on_device(): lax.all_to_all(spectra.reshape(groups, pairs, 128), 'gx', split_axis=0, c...  10 us
    mul x1, local copies, waits for them, and re-layouts, on_device(): pointwise_weight[:, None, :, None] * eye[None, :, None, :]  8.41 us
    all_to_all x1, starting transfers between devices, on_device(): lax.all_to_all(spectra.reshape(groups, pairs, 128), 'gx', split_axis=0, c...  7.38 us
    all_to_all x1, starting transfers between devices, on_device(): lax.all_to_all(grads.reshape(groups, count, 128), 'gx', split_axis=0, con...  3.51 us
    mul x1, other arithmetic, on_device(): pointwise_weight[:, None, :, None] * eye[None, :, None, :]  2.29 us
    unnamed x8, local copies, waits for them, and re-layouts  1.99 us
    squeeze x1, local copies, waits for them, and re-layouts, on_device(): other = lax.dynamic_index_in_dim(modes, 1 - me, 0, keepdims=False)  1.65 us
  transfers between devices with their start and end apart: 3, of which 1 were waited for; matrix products, arithmetic and copies ran while one was open for 21% of the time, Pallas kernels for 8%

profile of v1, /device:TPU:0, one launch (start us, length us, event | category | flops | bytes accessed | tf_op | source)
XLA Modules:
  0.0 58.7 jit_solution(13049169906019512958)
XLA Ops:
  0.6 6.0 %shard_map.149 = f32[512,128]{1,0:T(8,128)} custom-call(f32[64,256]{1,0:T(8,128)} %constant.36.clone.scale_ref, bf16[32,128,128]{2,1,0:T(8,128)(2,1)} %bitcast.15, bf16[32,128,128]{2,1,0:T(8,128)(2,1)} %bitcast.13, bf16[128,128]{1,0:T(8,128)(2,1)} %constant.37.clone.fy_ref, bf16[2,8,256,256]{3,2,1,0:T(8,128)(2,1)} %constant.38.clone.fz_ref), custom_call_target="tpu_custom_call" | custom-call | flops 1000000000 | bytes 5000000 | tf_op jit(solution)/shard_map/pallas_call | solution.py:281
  6.6 7.4 %all-to-all-start = ((f32[16,32,128]{2,1,0:T(8,128)}), f32[16,32,128]{2,1,0:T(8,128)S(1)}, u32[]{:S(2)}, u32[]{:S(2)}) async-start(f32[16,32,128]{2,1,0:T(8,128)} %bitcast.17), calls=%async_computation | async-start | bytes 524288 | tf_op jit(solution)/shard_map/all_to_all | solution.py:329
  14.0 10.0 %all-to-all-done = f32[16,32,128]{2,1,0:T(8,128)S(1)} async-done(((f32[16,32,128]{2,1,0:T(8,128)}), f32[16,32,128]{2,1,0:T(8,128)S(1)}, u32[]{:S(2)}, u32[]{:S(2)}) %all-to-all-start) | async-done | bytes 262176 | tf_op jit(solution)/shard_map/all_to_all | solution.py:329
  24.0 0.0 copy-start.1
  24.0 0.7 %copy-done.1 = f32[16,32,128]{2,1,0:T(8,128)} copy-done((f32[16,32,128]{2,1,0:T(8,128)}, f32[16,32,128]{2,1,0:T(8,128)S(1)}, u32[]{:S(2)}) %copy-start.1) | copy-done | bytes 262168
  24.7 0.0 copy-start.2
  24.7 5.1 %shard_map.150 = (f32[2,32,8,128]{3,2,1,0:T(8,128)}, f32[256,128]{1,0:T(8,128)}) custom-call(f32[512,128]{1,0:T(8,128)} %bitcast.19, bf16[32,16,2048]{2,1,0:T(8,128)(2,1)} %weight_ref.1, bf16[16,96]{1,0:T(8,128)(2,1)} %constant.39.clone.fx_ref.ix_ref, bf16[16,96]{1,0:T(8,128)(2,1)} %constant.39.clone.fx_ref.ix_ref, ...), custom_call_target="tpu_custom_call" | custom-call | flops 1000000000 | bytes 4000000 | tf_op jit(solution)/shard_map/pallas_call | solution.py:281
  29.8 3.5 %all-to-all-start.1 = ((f32[16,16,128]{2,1,0:T(8,128)}), f32[16,16,128]{2,1,0:T(8,128)S(1)}, u32[]{:S(2)}, u32[]{:S(2)}) async-start(f32[16,16,128]{2,1,0:T(8,128)} %bitcast.20), calls=%async_computation.1 | async-start | bytes 262144 | tf_op jit(solution)/shard_map/all_to_all | solution.py:344
  33.3 1.6 %dynamic-slice_bitcast_fusion = (f32[32,8,128]{2,1,0:T(8,128)S(1)}, f32[32,8,128]{2,1,0:T(8,128)}) fusion(f32[2,32,8,128]{3,2,1,0:T(8,128)} %get-tuple-element.5, s32[]{:T(128)S(6)} %select_n.8, s32[]{:T(128)S(6)} %select_n.7), kind=kLoop, calls=%fused_computation.1 | loop fusion | bytes 524296 | tf_op jit(solution)/shard_map/jit(dynamic_index_in_dim)/squeeze | solution.py:350
  35.0 1.5 %collective-permute-start = (f32[32,8,128]{2,1,0:T(8,128)S(1)}, f32[32,8,128]{2,1,0:T(8,128)S(1)}, u32[]{:S(2)}, u32[]{:S(2)}) collective-permute-start(f32[32,8,128]{2,1,0:T(8,128)S(1)} %get-tuple-element.6), channel_id=1, source_target_pairs={{0,16},{16,0},{1,17},{17,1},{2,18},{18,2},{3,19},{19,3},{4,20},{20... | collective-permute-start | bytes 393224 | tf_op jit(solution)/shard_map/ppermute | solution.py:351
  36.5 0.0 copy-done.2
  36.5 2.3 %broadcast_multiply_fusion = bf16[32,16,32,16]{3,2,1,0:T(8,128)(2,1)} fusion(bf16[16,16]{1,0:T(8,128)(2,1)S(1)} %fusion, bf16[32,32]{1,0:T(8,128)(2,1)S(1)} %copy-done.2), kind=kLoop, calls=%fused_computation | loop fusion | flops 262144 | bytes 526848 | tf_op jit(solution)/shard_map/mul | solution.py:364
  38.8 8.4 %mul.20.mix_ref = bf16[512,512]{1,0:T(8,128)(2,1)} reshape(bf16[32,16,32,16]{3,2,1,0:T(8,128)(2,1)} %broadcast_multiply_fusion) | data formatting | bytes 1048576 | tf_op jit(solution)/shard_map/mul | solution.py:364
  47.2 0.0 collective-permute-done.other_ref
  47.2 0.0 copy-start.3
  47.2 0.6 %copy-done.3 = f32[32,8,128]{2,1,0:T(8,128)} copy-done((f32[32,8,128]{2,1,0:T(8,128)}, f32[32,8,128]{2,1,0:T(8,128)S(1)}, u32[]{:S(2)}) %copy-start.3) | copy-done | bytes 131096
  47.8 4.9 %shard_map.152 = f32[32,8,2048]{2,1,0:T(8,128)} custom-call(f32[32,8,128]{2,1,0:T(8,128)} %get-tuple-element.7.mine_ref, f32[32,8,128]{2,1,0:T(8,128)} %copy-done.3, bf16[256,2304]{1,0:T(8,128)(2,1)} %constant.42.clone.repeat_ref), custom_call_target="tpu_custom_call" | custom-call | flops 1000000000 | bytes 3000000 | tf_op jit(solution)/shard_map/pallas_call | solution.py:281
  52.8 0.0 all-to-all-done.1
  52.8 0.0 copy-start
  52.8 0.6 %copy-done = f32[16,16,128]{2,1,0:T(8,128)} copy-done((f32[16,16,128]{2,1,0:T(8,128)}, f32[16,16,128]{2,1,0:T(8,128)S(1)}, u32[]{:S(2)}) %copy-start) | copy-done | bytes 131096
  53.4 5.3 %shard_map.151 = bf16[32,128,128]{2,1,0:T(8,128)(2,1)} custom-call(f32[256,128]{1,0:T(8,128)} %bitcast.18, bf16[32,128,128]{2,1,0:T(8,128)(2,1)} %bitcast.14, bf16[512,512]{1,0:T(8,128)(2,1)} %mul.20.mix_ref, bf16[2,256,2048]{2,1,0:T(8,128)(2,1)} %constant.43.clone.iz_ref, bf16[128,192]{1,0:T(8,128)(2,1)} %constant.44.clone.iy_ref), custom_call_target="tpu_custom_call" | custom-call | flops 1000000000 | bytes 4000000 | tf_op jit(solution)/shard_map/pallas_call | solution.py:281
  (1 shorter events, 0.0 us)
Async XLA Ops:
  6.6 17.4 %all-to-all-start = ((f32[16,32,128]{2,1,0:T(8,128)}), f32[16,32,128]{2,1,0:T(8,128)S(1)}, u32[]{:S(2)}, u32[]{:S(2)}) async-start(f32[16,32,128]{2,1,0:T(8,128)} %bitcast.17), calls=%async_computation | async-start | bytes 524288 | tf_op jit(solution)/shard_map/all_to_all | solution.py:329
  24.0 0.7 %copy-start.1 = (f32[16,32,128]{2,1,0:T(8,128)}, f32[16,32,128]{2,1,0:T(8,128)S(1)}, u32[]{:S(2)}) copy-start(f32[16,32,128]{2,1,0:T(8,128)S(1)} %all-to-all-done) | copy-start | bytes 786436
  24.7 11.7 %copy-start.2 = (bf16[32,32]{1,0:T(8,128)(2,1)S(1)}, bf16[32,32]{1,0:T(8,128)(2,1)}, u32[]{:S(2)}) copy-start(bf16[32,32]{1,0:T(8,128)(2,1)} %param.17) | copy-start | bytes 6148
  29.8 23.0 %all-to-all-start.1 = ((f32[16,16,128]{2,1,0:T(8,128)}), f32[16,16,128]{2,1,0:T(8,128)S(1)}, u32[]{:S(2)}, u32[]{:S(2)}) async-start(f32[16,16,128]{2,1,0:T(8,128)} %bitcast.20), calls=%async_computation.1 | async-start | bytes 262144 | tf_op jit(solution)/shard_map/all_to_all | solution.py:344
  35.0 12.2 %collective-permute-start = (f32[32,8,128]{2,1,0:T(8,128)S(1)}, f32[32,8,128]{2,1,0:T(8,128)S(1)}, u32[]{:S(2)}, u32[]{:S(2)}) collective-permute-start(f32[32,8,128]{2,1,0:T(8,128)S(1)} %get-tuple-element.6), channel_id=1, source_target_pairs={{0,16},{16,0},{1,17},{17,1},{2,18},{18,2},{3,19},{19,3},{4,20},{20... | collective-permute-start | bytes 393224 | tf_op jit(solution)/shard_map/ppermute | solution.py:351
  47.2 0.6 %copy-start.3 = (f32[32,8,128]{2,1,0:T(8,128)}, f32[32,8,128]{2,1,0:T(8,128)S(1)}, u32[]{:S(2)}) copy-start(f32[32,8,128]{2,1,0:T(8,128)S(1)} %collective-permute-done.other_ref) | copy-start | bytes 393220
  52.8 0.6 %copy-start = (f32[16,16,128]{2,1,0:T(8,128)}, f32[16,16,128]{2,1,0:T(8,128)S(1)}, u32[]{:S(2)}) copy-start(f32[16,16,128]{2,1,0:T(8,128)S(1)} %all-to-all-done.1) | copy-start | bytes 393220

commit v2 on v1

v2 whole, which is shorter than its diff:
```python
import functools
import math

import jax
import jax.numpy as jnp
import ml_dtypes
import numpy as np
from jax import lax
from jax.experimental import pallas as pl
from jax.experimental.pallas import tpu as pltpu
from jax.sharding import PartitionSpec as P

M = 16
F32 = jnp.float32
BF16 = jnp.bfloat16
MIB = 1024 * 1024
ROWS = 3 * M


def kept_freqs(half_count, length):
    index = np.arange(2 * half_count)
    return np.where(index < half_count, index, index + length - 2 * half_count)


def phases(frequency, length):
    product = np.outer(frequency, np.arange(length)) % length
    angle = product * (2.0 * math.pi / length)
    return np.cos(angle), np.sin(angle)


def split_np(table):
    high = table.astype(ml_dtypes.bfloat16)
    low = (table - high.astype(np.float64)).astype(ml_dtypes.bfloat16)
    return high, low


def split(value):
    high = value.astype(BF16)
    low = (value - high.astype(F32)).astype(BF16)
    return high, low


def dot(left, right):
    return jnp.dot(left, right, preferred_element_type=F32)


def forward_tables(length_y, length_z):
    cos_y, sin_y = phases(np.arange(M + 1), length_y)
    rows = np.zeros((ROWS, length_y))
    rows[:M], rows[M : 2 * M] = cos_y[:M], -sin_y[:M]
    rows[2 * M], rows[2 * M + 1] = cos_y[M], -sin_y[M]
    along_y = np.concatenate(split_np(rows), 1)
    cos_z, sin_z = phases(np.arange(M), length_z)
    along_z = np.concatenate([np.tile(cos_z.T, (1, 8)), np.tile(sin_z.T, (1, 8))], 1)
    return along_y, np.stack(split_np(along_z))


def inverse_tables(length_y, length_z):
    cos_z, sin_z = phases(np.arange(M), length_z)
    along_z = np.zeros((2, 2, 8, M, 2, length_z))
    for place in range(8):
        along_z[0, 0, place, :, place % 2] = cos_z
        along_z[0, 1, place, :, place % 2] = -sin_z
        along_z[1, 0, place, :, place % 2] = sin_z
        along_z[1, 1, place, :, place % 2] = cos_z
    along_z = along_z.reshape(2, 2 * 8 * M, 2 * length_z)
    along_z = np.stack([np.stack(split_np(part)) for part in along_z])
    cos_y, sin_y = phases(np.arange(M + 1), length_y)
    columns = np.zeros((length_y, ROWS))
    for k in range(M + 1):
        columns[:, mode_row(0, k)] = cos_y[k]
        columns[:, mode_row(1, k)] = -sin_y[k]
    high, low = split_np(columns)
    return along_z, np.concatenate([high, high, low], 1)


def mode_row(part, k):
    return 2 * M + part if k == M else part * M + k


def x_tables(kept_x, width_x):
    cos_x, sin_x = phases(kept_freqs(kept_x // 2, width_x), width_x)
    high, low = split_np(np.concatenate([cos_x, sin_x], 1))
    forward = np.concatenate([high, high, low], 1)
    high, low = split_np(np.concatenate([cos_x.T, sin_x.T], 1))
    inverse = np.concatenate([high, high, low], 1)
    return forward, inverse


def spread_table(channels):
    copies = 128 // channels
    table = np.zeros((2, 2, 2, channels, 2, copies, channels))
    eye = np.eye(channels)
    for part in range(2):
        table[:, part, 1, :, part] = eye[:, None, :]
    return table.reshape(8 * channels, 256).astype(ml_dtypes.bfloat16)


def gather_table(channels):
    table = np.zeros((2, channels, channels, 2, 2, 2, channels))
    for i in range(channels):
        table[0, i, :, 0, :, 0, i] = 1.0
        table[1, i, :, 0, :, 1, i] = 1.0
        table[1, i, :, 1, :, 0, i] = -1.0
        table[0, i, :, 1, :, 1, i] = 1.0
    return table.reshape(2 * channels * channels, 8 * channels).astype(ml_dtypes.bfloat16)


def repeat_table(channels):
    square = channels * channels
    table = np.zeros((2, 2, channels, 2 * square + 256))
    for i in range(channels):
        for part in range(2):
            start = part * square + i * channels
            table[part, 0, i, start : start + channels] = 1.0
            table[part, 1, i, 2 * square + part * 128 + i : 2 * square + part * 128 + 128 : channels] = 1.0
    return table.reshape(4 * channels, -1).astype(ml_dtypes.bfloat16)


def forward_kernel(
    field_hbm, cot_hbm, scale_hbm, fy_hbm, fz_hbm,
    out_ref, data_ref, scale_ref, fy_ref, fz_ref, rows_ref, sems,
):
    channels, _, length_z = field_hbm.shape
    copies = []

    def start(source, target):
        copy = pltpu.make_async_copy(source, target, sems.at[len(copies)])
        copy.start()
        copies.append(copy)
        return copy

    half = channels // 2
    table_y = start(fy_hbm, fy_ref)
    chunks = []
    for array, ref in enumerate((field_hbm, cot_hbm)):
        for first in (0, half):
            part = pl.ds(first, half)
            chunks.append((array, first, start(ref.at[part], data_ref.at[array, part])))
        if array == 0:
            table_z = start(fz_hbm, fz_ref)
            table_scale = start(scale_hbm, scale_ref)
    table_y.wait()
    for array, first, copy in chunks:
        copy.wait()
        for pair in range(first // 2, (first + half) // 2):
            data = jnp.concatenate([data_ref[array, 2 * pair], data_ref[array, 2 * pair + 1]], axis=1)
            value = dot(fy_ref[...], jnp.concatenate([data, data], axis=0))
            base = (array * channels + 2 * pair) * ROWS
            rows_ref[base : base + ROWS, :] = value[:, :length_z]
            rows_ref[base + ROWS : base + 2 * ROWS, :] = value[:, length_z:]
    table_z.wait()
    table_scale.wait()
    count = 2 * channels
    group = lax.broadcasted_iota(jnp.int32, (16, 256), 1) // M % 8
    lefts, rights = [], []
    for place in range(8):
        keep = jnp.where(group == place, 1.0, 0.0).astype(BF16)
        keep = jnp.concatenate([keep] * (length_z // 16), axis=0)
        table_high, table_low = fz_ref[0] * keep, fz_ref[1] * keep
        sources = [part * M + octet * 8 + place for part in range(2) for octet in range(2)]
        if place == 0:
            sources += [2 * M, 2 * M + 1]
        rows = [rows_ref[pl.ds(source, count, stride=ROWS), :] for source in sources]
        high, low = split(jnp.concatenate(rows, axis=0))
        left = jnp.concatenate([high, low, high], axis=1)
        right = jnp.concatenate([table_high, table_high, table_low], axis=0)
        if place == 0:
            last = dot(left[4 * count :], right)
            left = left[: 4 * count]
        lefts.append(left)
        rights.append(right)
    total = dot(jnp.concatenate(lefts, axis=1), jnp.concatenate(rights, axis=0))

    def turned(real, imag, sign):
        if sign > 0:
            block = (real[:, :128] + imag[:, 128:], imag[:, :128] - real[:, 128:])
        else:
            block = (real[:, :128] - imag[:, 128:], -imag[:, :128] - real[:, 128:])
        scaled = []
        for part in block:
            scaled += [part[:channels], part[channels:] * scale_ref[...]]
        return jnp.concatenate(scaled, axis=0).T

    for octet in range(2):
        real = total[octet * count : (octet + 1) * count]
        imag = total[(2 + octet) * count : (3 + octet) * count]
        out_ref[octet * 128 : (octet + 1) * 128, :] = turned(real, imag, 1)
        minus = turned(real, imag, -1)
        for place in range(8):
            k = octet * 8 + place
            if k > 0:
                out_ref[(2 * M - k) * M : (2 * M - k + 1) * M, :] = minus[place * M : (place + 1) * M]
    out_ref[M * M : (M + 1) * M, :] = turned(last[:count], last[count:], -1)[:M]


def mid_kernel(
    samples, planes_ref, weight_ref, fx_ref, ix_ref, spread_ref, gather_ref,
    mine_ref, other_ref, out_ref, rows_ref, high_ref, low_ref,
):
    pairs, kept_x, _ = weight_ref.shape
    width_x = planes_ref.shape[0] // pairs
    pack = width_x * pairs // out_ref.shape[0]
    share = kept_x // samples
    me = lax.axis_index("dp")
    lane = lax.broadcasted_iota(jnp.int32, (width_x, 128), 1)
    sign = jnp.where(lane < 64, 1.0, -1.0).astype(F32)
    for step in range(pairs // 2):
        columns = []
        for q in (2 * step, 2 * step + 1):
            plane = planes_ref[pl.ds(q, width_x, stride=pairs), :]
            turned = pltpu.roll(plane, 64, 1) * sign
            columns.append(jnp.concatenate([plane, turned], axis=0))
        high, low = split(jnp.concatenate(columns, axis=1))
        modes = dot(fx_ref[...], jnp.concatenate([high, low, high], axis=0))
        for index, q in enumerate((2 * step, 2 * step + 1)):
            mode = modes[:, index * 128 : (index + 1) * 128]
            rows_ref[q * kept_x : (q + 1) * kept_x, :] = mode
            for ahead in range(samples):
                start = q * kept_x + lax.rem(me + ahead, samples) * share
                part = rows_ref[pl.ds(pl.multiple_of(start, share), share), :]
                if ahead == 0:
                    mine_ref[q] = part
                else:
                    other_ref[(ahead - 1) * pairs + q] = part
    square = weight_ref.shape[2] // 2
    high, low = split(rows_ref[...])
    spread = dot(jnp.concatenate([high, low], axis=1), spread_ref[...])
    for q in range(pairs):
        rows = slice(q * kept_x, (q + 1) * kept_x)
        real, imag = spread[rows, :128], spread[rows, 128:]
        for start in range(0, square, 128):
            w_real = weight_ref[q, :, start : start + 128].astype(F32)
            w_imag = weight_ref[q, :, square + start : square + start + 128].astype(F32)
            first = split(real * w_real + imag * w_imag)
            second = split(imag * w_real - real * w_imag)
            high_ref[rows, start : start + 128] = first[0]
            low_ref[rows, start : start + 128] = first[1]
            high_ref[rows, square + start : square + start + 128] = second[0]
            low_ref[rows, square + start : square + start + 128] = second[1]
    grads = dot(high_ref[...], gather_ref[...]) + dot(low_ref[...], gather_ref[...])
    count = pairs // pack
    if pack == 2:
        size = count * kept_x
        lane = lax.broadcasted_iota(jnp.int32, (size, 256), 1) % 128
        grads = jnp.where(lane < 64, grads[:size], grads[size:])
    for step in range(count // 2):
        columns = []
        for row in (2 * step, 2 * step + 1):
            block = grads[row * kept_x : (row + 1) * kept_x]
            columns.append(jnp.concatenate([block[:, :128], block[:, 128:]], axis=0))
        high, low = split(jnp.concatenate(columns, axis=1))
        planes = dot(ix_ref[...], jnp.concatenate([high, low, high], axis=0))
        for index, row in enumerate((2 * step, 2 * step + 1)):
            out_ref[pl.ds(row, width_x, stride=count), :] = planes[:, index * 128 : (index + 1) * 128]


def weight_kernel(modes_ref, repeat_ref, *refs):
    out_ref = refs[-1]
    pairs, share, _ = modes_ref.shape
    square = out_ref.shape[2] // 2
    chunk = min(pairs, 8)

    @pl.loop(0, pairs // chunk)
    def _(step):
        part = pl.ds(step * chunk, chunk)
        high, low = split(modes_ref[part].reshape(chunk * share, 128))
        side = jnp.concatenate([high, low], axis=1)

        def repeated(start):
            table = repeat_ref[:, start : start + 256]
            return dot(side, jnp.concatenate([table, table], axis=0))

        cots = repeated(2 * square)
        c_real = jnp.concatenate([cots[:, :128]] * 2, axis=1)
        c_imag = jnp.concatenate([cots[:, 128:]] * 2, axis=1)
        for start in range(0, square, 256):
            f_real, f_imag = repeated(start), repeated(square + start)
            real = f_real * c_real + f_imag * c_imag
            imag = f_real * c_imag - f_imag * c_real
            for first, value in ((start, real), (square + start, imag)):
                value = value.reshape(chunk, share, 256)
                for before_ref in refs[:-1]:
                    value = value + before_ref[part, :, first : first + 256]
                out_ref[part, :, first : first + 256] = value


def linear_kernel(cot_ref, weight_ref, linear_ref, mix_ref):
    channels, length_y, length_z = cot_ref.shape
    size = 16 * channels
    left = lax.broadcasted_iota(jnp.int32, (size, channels), 0) // 16 == lax.broadcasted_iota(
        jnp.int32, (size, channels), 1
    )
    right = lax.broadcasted_iota(jnp.int32, (channels, size), 1) // 16 == lax.broadcasted_iota(
        jnp.int32, (channels, size), 0
    )
    tall = dot(left.astype(F32).astype(BF16), weight_ref[...]).astype(BF16)
    wide = dot(tall, right.astype(F32).astype(BF16))
    same = lax.broadcasted_iota(jnp.int32, (size, size), 0) % 16 == lax.broadcasted_iota(
        jnp.int32, (size, size), 1
    ) % 16
    mix_ref[...] = jnp.where(same, wide, 0.0).astype(BF16)
    for step in range(length_y // 32):
        columns = []
        for part in range(2):
            first = step * 32 + part * 16
            columns.append(cot_ref[:, first : first + 16, :].reshape(channels * 16, length_z))
        mixed = dot(mix_ref[...], jnp.concatenate(columns, axis=1))
        for part in range(2):
            first = step * 32 + part * 16
            linear_ref[:, first : first + 16, :] = mixed[:, part * length_z : (part + 1) * length_z].reshape(
                channels, 16, length_z
            )


def inverse_kernel(planes_ref, linear_ref, iz_ref, iy_ref, out_ref, rows_ref):
    channels, _, length_z = linear_ref.shape
    rows = planes_ref.shape[0]
    pack = 2 * M * M // rows
    group = lax.broadcasted_iota(jnp.int32, (16, 256), 1) // M % 8
    keeps = []
    for step in range(4):
        keep = jnp.where(group // 2 == step, 1.0, 0.0).astype(BF16)
        keeps.append(jnp.concatenate([keep] * (channels // 16), axis=0))
    lane = lax.broadcasted_iota(jnp.int32, (M, 128), 1)

    def block(index):
        return planes_ref[index * M : (index + 1) * M, :]

    def halves(turned):
        found = []
        for low_bit in range(pack):
            first = low_bit * 2 * channels
            found.append(
                jnp.concatenate(
                    [turned[first : first + channels], turned[first + channels : first + 2 * channels]], axis=1
                )
            )
        return found

    def along_z(parts, which, steps):
        terms = [split(part) for part in parts]
        left = []
        for step in steps:
            for high, low in terms:
                high, low = high * keeps[step], low * keeps[step]
                left.append(jnp.concatenate([high, low, high], axis=1))
        right = jnp.concatenate([iz_ref[which, 0], iz_ref[which, 0], iz_ref[which, 1]], axis=0)
        return dot(jnp.concatenate(left, axis=0), right)

    def put(value, part, k):
        first = mode_row(part, k) * channels
        rows_ref[first : first + channels, :] = value

    blocks = rows // M
    octets = blocks // 16
    for octet in range(octets):
        sums, differences = [], []
        for place in range(8):
            index = octet * 8 + place
            plus = block(index)
            minus = block(blocks - index) if index > 0 else jnp.zeros_like(plus)
            if pack == 2:
                minus = jnp.where(lane < 64, minus, block(blocks - 1 - index))
            sums.append(plus + minus)
            differences.append(plus - minus)
        for part, stack in enumerate((sums, differences)):
            parts = halves(jnp.concatenate(stack, axis=0).T)
            value = along_z(parts, part, range(4))
            for step in range(4):
                for low_bit in range(pack):
                    first = (step * pack + low_bit) * channels
                    for parity in range(2):
                        k = (octet * 8 + step * 2 + parity) * pack + low_bit
                        put(
                            value[first : first + channels, parity * length_z : (parity + 1) * length_z],
                            part,
                            k,
                        )
    last = block(blocks // 2)
    last = jnp.concatenate([last, jnp.zeros((128 - M, 128), F32)], axis=0).T
    first_half = halves(last)[:1]
    put(along_z(first_half, 0, [0])[:, :length_z], 0, M)
    put(-along_z(first_half, 1, [0])[:, :length_z], 1, M)
    rows_ref[(2 * M + 2) * channels :, :] = jnp.zeros(((ROWS - 2 * M - 2) * channels, length_z), F32)
    for pair in range(channels // 2):
        columns = [rows_ref[pl.ds(2 * pair + side, ROWS, stride=channels), :] for side in range(2)]
        high, low = split(jnp.concatenate(columns, axis=1))
        value = dot(iy_ref[...], jnp.concatenate([high, low, high], axis=0))
        for side in range(2):
            channel = 2 * pair + side
            spectral = value[:, side * length_z : (side + 1) * length_z]
            out_ref[channel] = (spectral + linear_ref[channel]).astype(BF16)


def call(kernel, out_shape, scratch, limit, flops, moved, *args, in_specs=None):
    kwargs = {} if in_specs is None else {"in_specs": in_specs}
    return pl.pallas_call(
        kernel,
        out_shape=out_shape,
        **kwargs,
        scratch_shapes=scratch,
        compiler_params=pltpu.CompilerParams(vmem_limit_bytes=limit * MIB),
        cost_estimate=pl.CostEstimate(flops=flops, bytes_accessed=moved, transcendentals=0),
    )(*args)


def weight_terms(modes, channels):
    parts = modes.reshape(modes.shape[:3] + (2, 2, channels))
    in_real, in_imag = parts[..., 0, 0, :, None], parts[..., 1, 0, :, None]
    cot_real, cot_imag = parts[..., 0, 1, None, :], parts[..., 1, 1, None, :]
    real = jnp.sum(in_real * cot_real + in_imag * cot_imag, axis=0)
    imag = jnp.sum(in_real * cot_imag - in_imag * cot_real, axis=0)
    stacked = jnp.stack([real, imag], axis=2)
    return stacked.reshape(stacked.shape[:2] + (-1,))


def on_device(field, cotangent, spectral_weight, pointwise_weight):
    _, planes, channels, length_y, length_z = field.shape
    pairs, kept_x, _ = spectral_weight.shape
    groups = lax.axis_size("gx")
    samples = lax.axis_size("dp")
    width_x = planes * groups
    share = kept_x // samples
    pack = 2 if pairs == 2 * M else 1
    count = pairs // pack
    all_pairs = 2 * M * M
    cells = width_x * length_y * length_z
    shape = jax.ShapeDtypeStruct
    field = field.reshape(channels, length_y, length_z)
    cotangent = cotangent.reshape(channels, length_y, length_z)

    fy, fz = forward_tables(length_y, length_z)
    iz, iy = inverse_tables(length_y, length_z)
    fx, ix = x_tables(kept_x, width_x)
    scale = np.where(np.arange(M) == 0, 1.0, 2.0) / cells
    scale = np.tile(scale, 8).astype(np.float32)[None]

    spectra = call(
        forward_kernel,
        shape((all_pairs, 128), F32),
        [
            pltpu.VMEM((2,) + field.shape, BF16),
            pltpu.VMEM(scale.shape, F32),
            pltpu.VMEM(fy.shape, BF16),
            pltpu.VMEM(fz.shape, BF16),
            pltpu.VMEM((2 * channels * ROWS, length_z), F32),
            pltpu.SemaphoreType.DMA((7,)),
        ],
        58, 10**9, 5 * 10**6,
        field, cotangent, scale, fy, fz,
        in_specs=[pl.BlockSpec(memory_space=pltpu.HBM)] * 5,
    )
    received = lax.all_to_all(
        spectra.reshape(groups, pairs, 128), "gx", split_axis=0, concat_axis=0, tiled=True
    )
    mine, other, grads = call(
        functools.partial(mid_kernel, samples),
        (
            shape((pairs, share, 128), F32),
            shape((pairs * (samples - 1), share, 128), F32),
            shape((width_x * count, 128), F32),
        ),
        [
            pltpu.VMEM((pairs * kept_x, 128), F32),
            pltpu.VMEM((pairs * kept_x, 2 * channels * channels), BF16),
            pltpu.VMEM((pairs * kept_x, 2 * channels * channels), BF16),
        ],
        16, 10**9, 4 * 10**6,
        received.reshape(width_x * pairs, 128), spectral_weight, fx, ix,
        spread_table(channels), gather_table(channels),
    )
    grads, late_cotangent = lax.optimization_barrier((grads, cotangent))
    linear = call(
        linear_kernel,
        shape((channels, length_y, length_z), F32),
        [pltpu.VMEM((16 * channels, 16 * channels), BF16)],
        16, 2 * 10**9, 3 * 10**6,
        late_cotangent, pointwise_weight,
    )
    returned = lax.all_to_all(
        grads.reshape(groups, count, 128), "gx", split_axis=0, concat_axis=0, tiled=True
    )
    repeat = repeat_table(channels)
    if samples == 2 and share % 8 == 0:
        other = lax.ppermute(other, "dp", [(0, 1), (1, 0)])
        weight_grad = []
        for modes in (mine, other):
            weight_grad = [
                call(
                    weight_kernel,
                    shape((pairs, share, 2 * channels * channels), F32),
                    [],
                    16, 2 * 10**9, 3 * 10**6,
                    modes, repeat, *weight_grad,
                )
            ]
        weight_grad = weight_grad[0]
    else:
        me = lax.axis_index("dp")
        modes = jnp.concatenate([mine[None], other.reshape(samples - 1, pairs, share, 128)])
        modes = jnp.roll(modes, me, 0)
        modes = lax.all_to_all(modes, "dp", split_axis=0, concat_axis=0, tiled=True)
        weight_grad = weight_terms(modes, channels)

    field_grad = call(
        inverse_kernel,
        shape((channels, length_y, length_z), BF16),
        [pltpu.VMEM((ROWS * channels, length_z), F32)],
        16, 10**9, 4 * 10**6,
        returned.reshape(width_x * count, 128), linear, iz, iy,
    )
    return field_grad.reshape(1, planes, channels, length_y, length_z), weight_grad


def solution(mesh):
    placed = (
        P("dp", "gx", None, None, None),
        P("dp", "gx", None, None, None),
        P("gx", None, None),
        P(),
    )
    return jax.shard_map(
        on_device,
        mesh=mesh,
        in_specs=placed,
        out_specs=(P("dp", "gx", None, None, None), P("gx", "dp", None)),
        check_vma=False,
    )
```

time: 59.1 us -> 40.1 us (0.68)
  blocking collectives: 0 us -> 17.4 us
  local copies, waits for them, and re-layouts: 12.1 us -> 1.4 us
  waiting for transfers between devices: 10 us -> 0.45 us
  starting transfers between devices: 12.4 us -> 5.07 us
  Pallas kernels: 21.3 us -> 14.7 us
  other arithmetic: 2.3 us -> 0 us
    all_to_all x0 -> x1, blocking collectives: none -> 17.4 us  [on_device(): lax.all_to_all(spectra.reshape(groups, pairs, 128), 'gx', split_axis=0, c...]
    all_to_all x1 -> x0, waiting for transfers between devices: 10 us -> none  [on_device(): lax.all_to_all(spectra.reshape(groups, pairs, 128), 'gx', split_axis=0, c...]
    mul x1 -> x0, local copies, waits for them, and re-layouts: 8.41 us -> none  [on_device(): pointwise_weight[:, None, :, None] * eye[None, :, None, :]]
    all_to_all x1 -> x0, starting transfers between devices: 7.38 us -> none  [on_device(): lax.all_to_all(spectra.reshape(groups, pairs, 128), 'gx', split_axis=0, c...]
    pallas_call x4 -> x6, Pallas kernels: 21.3 us -> 14.7 us  [call(): pl.pallas_call(kernel, out_shape=out_shape, **kwargs, scratch_shapes=scra...]
    mul x1 -> x0, other arithmetic: 2.29 us -> none  [on_device(): pointwise_weight[:, None, :, None] * eye[None, :, None, :]]
    squeeze x1 -> x0, local copies, waits for them, and re-layouts: 1.65 us -> none  [on_device(): other = lax.dynamic_index_in_dim(modes, 1 - me, 0, keepdims=False)]
    unnamed x8 -> x18, local copies, waits for them, and re-layouts: 1.99 us -> 1.4 us
  transfers between devices with their start and end apart: 3 -> 2, of which waited for: 1 -> 1; matrix products, arithmetic and copies ran while one was open for 21% -> 0% of each run, Pallas kernels for 8% -> 13%
where the time goes in v2:
time: 40.1 us; the launch traced here: 39.8 us
  blocking collectives  17.4 us (43%)
  Pallas kernels  14.7 us (37%)
  starting transfers between devices  5.07 us (13%)
  local copies, waits for them, and re-layouts  1.4 us (3%)
  between operations  0.73 us (2%)
  waiting for transfers between devices  0.45 us (1%)
    all_to_all x1, blocking collectives, on_device(): lax.all_to_all(spectra.reshape(groups, pairs, 128), 'gx', split_axis=0, c...  17.4 us
    pallas_call x6, Pallas kernels, call(): pl.pallas_call(kernel, out_shape=out_shape, **kwargs, scratch_shapes=scra...  14.7 us
    all_to_all x1, starting transfers between devices, on_device(): lax.all_to_all(grads.reshape(groups, count, 128), 'gx', split_axis=0, con...  3.51 us
    ppermute x1, starting transfers between devices, on_device(): other = lax.ppermute(other, 'dp', [(0, 1), (1, 0)])  1.56 us
    unnamed x18, local copies, waits for them, and re-layouts  1.4 us
  transfers between devices with their start and end apart: 2, of which 1 were waited for; matrix products, arithmetic and copies ran while one was open for 0% of the time, Pallas kernels for 13%

profile of v2, /device:TPU:0, one launch (start us, length us, event | category | flops | bytes accessed | tf_op | source)
XLA Modules:
  0.0 39.8 jit_solution(8723003992565548326)
XLA Ops:
  0.6 0.0 copy-start.2
  0.6 0.0 copy-start.5
  0.7 0.0 copy-start.7
  0.7 0.0 copy-start.8
  0.7 4.0 %shard_map.149 = f32[512,128]{1,0:T(8,128)} custom-call(bf16[32,128,128]{2,1,0:T(8,128)(2,1)} %bitcast.13, bf16[32,128,128]{2,1,0:T(8,128)(2,1)} %bitcast.9, f32[1,128]{1,0:T(1,128)} %constant.18.clone.scale_hbm, bf16[48,256]{1,0:T(8,128)(2,1)} %constant.19.clone.fy_hbm, bf16[2,128,256]{2,1,0:T(8,128)(2,1)} %constant.20.clone.fz_hbm), custom_call_target="tpu_custom_call" | custom-call | flops 1000000000 | bytes 5000000 | tf_op jit(solution)/shard_map/pallas_call | solution.py:398
  4.7 17.4 %all_to_all.10 = f32[16,32,128]{2,1,0:T(8,128)S(1)} all-to-all(f32[16,32,128]{2,1,0:T(8,128)} %bitcast.12), channel_id=1, replica_groups=mesh['dp'=2,'gx'=16] {'gx'}, dimensions={0} | all-to-all | bytes 524288 | tf_op jit(solution)/shard_map/all_to_all | solution.py:454
  22.1 0.0 copy-start.4
  22.1 0.0 copy-done.2
  22.1 0.0 copy-done.5
  22.1 0.0 copy-done.7
  22.1 0.0 copy-done.8
  22.1 3.5 %shard_map.150 = (f32[32,8,128]{2,1,0:T(8,128)S(1)}, f32[32,8,128]{2,1,0:T(8,128)S(1)}, f32[256,128]{1,0:T(8,128)}) custom-call(f32[512,128]{1,0:T(8,128)S(1)} %bitcast.8, bf16[32,16,2048]{2,1,0:T(8,128)(2,1)S(1)} %copy-done.2, bf16[16,96]{1,0:T(8,128)(2,1)S(1)} %copy-done.8, bf16[16,96]{1,0:T(8,128)(2,1)S(1)} %copy-done.8, bf16[256,256]{1,0:T(8,128)(2,1)S(1)} %copy-done.7, ...), custom_call_target="tpu_custom_call" | custom-call | flops 1000000000 | bytes 4000000 | tf_op jit(solution)/shard_map/pallas_call | solution.py:398
  25.7 3.5 %all-to-all-start.1 = ((f32[16,16,128]{2,1,0:T(8,128)}), f32[16,16,128]{2,1,0:T(8,128)S(1)}, u32[]{:S(2)}, u32[]{:S(2)}) async-start(f32[16,16,128]{2,1,0:T(8,128)} %bitcast.4), calls=%async_computation.1 | async-start | bytes 262144 | tf_op jit(solution)/shard_map/all_to_all | solution.py:481
  29.2 1.6 %collective-permute-start = (f32[32,8,128]{2,1,0:T(8,128)S(1)}, f32[32,8,128]{2,1,0:T(8,128)S(1)}, u32[]{:S(2)}, u32[]{:S(2)}) collective-permute-start(f32[32,8,128]{2,1,0:T(8,128)S(1)} %get-tuple-element.10), channel_id=1, source_target_pairs={{0,16},{16,0},{1,17},{17,1},{2,18},{18,2},{3,19},{19,3},{4,20},{20... | collective-permute-start | bytes 393224 | tf_op jit(solution)/shard_map/ppermute | solution.py:486
  30.7 0.0 copy-done.4
  30.7 0.0 copy-start.3
  30.7 1.2 %copy-done.3 = bf16[1,1,32,128,128]{4,3,2,1,0:T(8,128)(2,1)S(1)} copy-done((bf16[1,1,32,128,128]{4,3,2,1,0:T(8,128)(2,1)S(1)}, bf16[1,1,32,128,128]{4,3,2,1,0:T(8,128)(2,1)}, u32[]{:S(2)}) %copy-start.3) | copy-done | bytes 1048600
  32.0 0.0 copy-start.6
  32.0 0.9 %shard_map.151.linear_ref = f32[32,128,128]{2,1,0:T(8,128)S(1)} custom-call(bf16[32,128,128]{2,1,0:T(8,128)(2,1)S(1)} %bitcast.10, bf16[32,32]{1,0:T(8,128)(2,1)S(1)} %copy-done.4), custom_call_target="tpu_custom_call" | custom-call | flops 2000000000 | bytes 3000000 | tf_op jit(solution)/shard_map/pallas_call | solution.py:398
  32.9 0.1 copy-done.6
  33.0 1.4 %shard_map.153.refs_0_ = f32[32,8,2048]{2,1,0:T(8,128)S(1)} custom-call(f32[32,8,128]{2,1,0:T(8,128)S(1)} %get-tuple-element.11.modes_ref, bf16[128,2304]{1,0:T(8,128)(2,1)S(1)} %copy-done.6), custom_call_target="tpu_custom_call" | custom-call | flops 2000000000 | bytes 3000000 | tf_op jit(solution)/shard_map/pallas_call | solution.py:398
  34.4 0.0 copy-start
  34.4 0.0 copy-start.1
  34.4 0.4 %collective-permute-done.modes_ref = f32[32,8,128]{2,1,0:T(8,128)S(1)} collective-permute-done((f32[32,8,128]{2,1,0:T(8,128)S(1)}, f32[32,8,128]{2,1,0:T(8,128)S(1)}, u32[]{:S(2)}, u32[]{:S(2)}) %collective-permute-start) | collective-permute-done | bytes 131104 | tf_op jit(solution)/shard_map/ppermute | solution.py:486
  34.9 2.7 %shard_map.154 = f32[32,8,2048]{2,1,0:T(8,128)} custom-call(f32[32,8,128]{2,1,0:T(8,128)S(1)} %collective-permute-done.modes_ref, bf16[128,2304]{1,0:T(8,128)(2,1)S(1)} %copy-done.6, f32[32,8,2048]{2,1,0:T(8,128)S(1)} %shard_map.153.refs_0_), custom_call_target="tpu_custom_call" | custom-call | flops 2000000000 | bytes 3000000 | tf_op jit(solution)/shard_map/pallas_call | solution.py:398
  37.6 0.0 all-to-all-done.1
  37.6 0.0 copy-done
  37.6 0.0 copy-done.1
  37.6 2.2 %shard_map.152 = bf16[32,128,128]{2,1,0:T(8,128)(2,1)} custom-call(f32[256,128]{1,0:T(8,128)S(1)} %bitcast.7, f32[32,128,128]{2,1,0:T(8,128)S(1)} %shard_map.151.linear_ref, bf16[2,2,256,256]{3,2,1,0:T(8,128)(2,1)S(1)} %copy-done, bf16[128,144]{1,0:T(8,128)(2,1)S(1)} %copy-done.1), custom_call_target="tpu_custom_call" | custom-call | flops 1000000000 | bytes 4000000 | tf_op jit(solution)/shard_map/pallas_call | solution.py:398
Async XLA Ops:
  0.6 21.5 %copy-start.2 = (bf16[32,16,2048]{2,1,0:T(8,128)(2,1)S(1)}, bf16[32,16,2048]{2,1,0:T(8,128)(2,1)}, u32[]{:S(2)}) copy-start(bf16[32,16,2048]{2,1,0:T(8,128)(2,1)} %weight_ref.2) | copy-start | bytes 6291460
  0.6 21.5 %copy-start.5 = (bf16[2048,256]{1,0:T(8,128)(2,1)S(1)}, bf16[2048,256]{1,0:T(8,128)(2,1)}, u32[]{:S(2)}) copy-start(bf16[2048,256]{1,0:T(8,128)(2,1)} %constant.23.clone.gather_ref) | copy-start | bytes 3145732
  0.7 21.5 %copy-start.7 = (bf16[256,256]{1,0:T(8,128)(2,1)S(1)}, bf16[256,256]{1,0:T(8,128)(2,1)}, u32[]{:S(2)}) copy-start(bf16[256,256]{1,0:T(8,128)(2,1)} %constant.22.clone.spread_ref) | copy-start | bytes 393220
  0.7 21.5 %copy-start.8 = (bf16[16,96]{1,0:T(8,128)(2,1)S(1)}, bf16[16,96]{1,0:T(8,128)(2,1)}, u32[]{:S(2)}) copy-start(bf16[16,96]{1,0:T(8,128)(2,1)} %constant.21.clone.fx_ref.ix_ref) | copy-start | bytes 9220
  22.1 8.6 %copy-start.4 = (bf16[32,32]{1,0:T(8,128)(2,1)S(1)}, bf16[32,32]{1,0:T(8,128)(2,1)}, u32[]{:S(2)}) copy-start(bf16[32,32]{1,0:T(8,128)(2,1)} %weight_ref.3) | copy-start | bytes 6148
  25.7 11.9 %all-to-all-start.1 = ((f32[16,16,128]{2,1,0:T(8,128)}), f32[16,16,128]{2,1,0:T(8,128)S(1)}, u32[]{:S(2)}, u32[]{:S(2)}) async-start(f32[16,16,128]{2,1,0:T(8,128)} %bitcast.4), calls=%async_computation.1 | async-start | bytes 262144 | tf_op jit(solution)/shard_map/all_to_all | solution.py:481
  29.2 5.7 %collective-permute-start = (f32[32,8,128]{2,1,0:T(8,128)S(1)}, f32[32,8,128]{2,1,0:T(8,128)S(1)}, u32[]{:S(2)}, u32[]{:S(2)}) collective-permute-start(f32[32,8,128]{2,1,0:T(8,128)S(1)} %get-tuple-element.10), channel_id=1, source_target_pairs={{0,16},{16,0},{1,17},{17,1},{2,18},{18,2},{3,19},{19,3},{4,20},{20... | collective-permute-start | bytes 393224 | tf_op jit(solution)/shard_map/ppermute | solution.py:486
  30.7 1.2 %copy-start.3 = (bf16[1,1,32,128,128]{4,3,2,1,0:T(8,128)(2,1)S(1)}, bf16[1,1,32,128,128]{4,3,2,1,0:T(8,128)(2,1)}, u32[]{:S(2)}) copy-start(bf16[1,1,32,128,128]{4,3,2,1,0:T(8,128)(2,1)} %param.15) | copy-start | bytes 3145732
  32.0 1.1 %copy-start.6 = (bf16[128,2304]{1,0:T(8,128)(2,1)S(1)}, bf16[128,2304]{1,0:T(8,128)(2,1)}, u32[]{:S(2)}) copy-start(bf16[128,2304]{1,0:T(8,128)(2,1)} %constant.24.clone.repeat_ref) | copy-start | bytes 1769476
  34.4 3.2 %copy-start = (bf16[2,2,256,256]{3,2,1,0:T(8,128)(2,1)S(1)}, bf16[2,2,256,256]{3,2,1,0:T(8,128)(2,1)}, u32[]{:S(2)}) copy-start(bf16[2,2,256,256]{3,2,1,0:T(8,128)(2,1)} %constant.25.clone.iz_ref) | copy-start | bytes 1572868
  34.4 3.2 %copy-start.1 = (bf16[128,144]{1,0:T(8,128)(2,1)S(1)}, bf16[128,144]{1,0:T(8,128)(2,1)}, u32[]{:S(2)}) copy-start(bf16[128,144]{1,0:T(8,128)(2,1)} %constant.26.clone.iy_ref) | copy-start | bytes 110596

commit v3 on v2

--- a/solution.py
+++ b/solution.py
@@ -97,13 +97,16 @@
 
 
 def gather_table(channels):
-    table = np.zeros((2, channels, channels, 2, 2, 2, channels))
-    for i in range(channels):
-        table[0, i, :, 0, :, 0, i] = 1.0
-        table[1, i, :, 0, :, 1, i] = 1.0
-        table[1, i, :, 1, :, 0, i] = -1.0
-        table[0, i, :, 1, :, 1, i] = 1.0
-    return table.reshape(2 * channels * channels, 8 * channels).astype(ml_dtypes.bfloat16)
+    square = channels * channels
+    table = np.zeros((2, square // 256, 128, 2, 2, 2, channels))
+    for pair in range(square // 256):
+        for lane in range(128):
+            i = (pair * 256 + (lane % 32 >= 16) * 128 + lane) // channels
+            table[0, pair, lane, 0, :, 0, i] = 1.0
+            table[1, pair, lane, 0, :, 1, i] = 1.0
+            table[1, pair, lane, 1, :, 0, i] = -1.0
+            table[0, pair, lane, 1, :, 1, i] = 1.0
+    return table.reshape(square, 8 * channels).astype(ml_dtypes.bfloat16)
 
 
 def repeat_table(channels):
@@ -196,7 +199,7 @@
 
 def mid_kernel(
     samples, planes_ref, weight_ref, fx_ref, ix_ref, spread_ref, gather_ref,
-    mine_ref, other_ref, out_ref, rows_ref, high_ref, low_ref,
+    mine_ref, other_ref, out_ref, rows_ref, split_ref,
 ):
     pairs, kept_x, _ = weight_ref.shape
     width_x = planes_ref.shape[0] // pairs
@@ -223,22 +226,43 @@
                     mine_ref[q] = part
                 else:
                     other_ref[(ahead - 1) * pairs + q] = part
+
     square = weight_ref.shape[2] // 2
-    high, low = split(rows_ref[...])
-    spread = dot(jnp.concatenate([high, low], axis=1), spread_ref[...])
-    for q in range(pairs):
-        rows = slice(q * kept_x, (q + 1) * kept_x)
-        real, imag = spread[rows, :128], spread[rows, 128:]
-        for start in range(0, square, 128):
-            w_real = weight_ref[q, :, start : start + 128].astype(F32)
-            w_imag = weight_ref[q, :, square + start : square + start + 128].astype(F32)
-            first = split(real * w_real + imag * w_imag)
-            second = split(imag * w_real - real * w_imag)
-            high_ref[rows, start : start + 128] = first[0]
-            low_ref[rows, start : start + 128] = first[1]
-            high_ref[rows, square + start : square + start + 128] = second[0]
-            low_ref[rows, square + start : square + start + 128] = second[1]
-    grads = dot(high_ref[...], gather_ref[...]) + dot(low_ref[...], gather_ref[...])
+    lane = lax.broadcasted_iota(jnp.int32, (kept_x, 128), 1) % 32
+    first_half = lane < 16
+
+    def halved(one, two):
+        kept = jnp.where(first_half, one, two)
+        moved = jnp.where(first_half, two, one)
+        return kept + jnp.where(first_half, pltpu.roll(moved, 112, 1), pltpu.roll(moved, 16, 1))
+
+    def products(rows, q, start):
+        real, imag = rows[:, :128], rows[:, 128:]
+        w_real = weight_ref[q, :, start : start + 128].astype(F32)
+        w_imag = weight_ref[q, :, square + start : square + start + 128].astype(F32)
+        return real * w_real + imag * w_imag, imag * w_real - real * w_imag
+
+    grads = []
+    chunk = 8
+    for first in range(0, pairs, chunk):
+        high, low = split(rows_ref[first * kept_x : (first + chunk) * kept_x, :])
+        spread = dot(jnp.concatenate([high, low], axis=1), spread_ref[...])
+        size = chunk * kept_x
+        base = 2 * first * kept_x
+        for place in range(chunk):
+            rows = spread[place * kept_x : (place + 1) * kept_x]
+            at = base + place * kept_x
+            for start in range(0, square, 256):
+                ones = products(rows, first + place, start)
+                twos = products(rows, first + place, start + 128)
+                for part in range(2):
+                    column = (part * square + start) // 2
+                    high, low = split(halved(ones[part], twos[part]))
+                    split_ref[at : at + kept_x, column : column + 128] = high
+                    split_ref[at + size : at + size + kept_x, column : column + 128] = low
+        both = dot(split_ref[base : base + 2 * size, :], gather_ref[...])
+        grads.append(both[:size] + both[size:])
+    grads = jnp.concatenate(grads, axis=0)
     count = pairs // pack
     if pack == 2:
         size = count * kept_x
@@ -255,37 +279,57 @@
             out_ref[pl.ds(row, width_x, stride=count), :] = planes[:, index * 128 : (index + 1) * 128]
 
 
-def weight_kernel(modes_ref, repeat_ref, *refs):
-    out_ref = refs[-1]
-    pairs, share, _ = modes_ref.shape
-    square = out_ref.shape[2] // 2
-    chunk = min(pairs, 8)
-
-    @pl.loop(0, pairs // chunk)
-    def _(step):
-        part = pl.ds(step * chunk, chunk)
-        high, low = split(modes_ref[part].reshape(chunk * share, 128))
-        side = jnp.concatenate([high, low], axis=1)
-
-        def repeated(start):
-            table = repeat_ref[:, start : start + 256]
-            return dot(side, jnp.concatenate([table, table], axis=0))
-
-        cots = repeated(2 * square)
-        c_real = jnp.concatenate([cots[:, :128]] * 2, axis=1)
-        c_imag = jnp.concatenate([cots[:, 128:]] * 2, axis=1)
-        for start in range(0, square, 256):
-            f_real, f_imag = repeated(start), repeated(square + start)
-            real = f_real * c_real + f_imag * c_imag
-            imag = f_real * c_imag - f_imag * c_real
-            for first, value in ((start, real), (square + start, imag)):
-                value = value.reshape(chunk, share, 256)
-                for before_ref in refs[:-1]:
-                    value = value + before_ref[part, :, first : first + 256]
-                out_ref[part, :, first : first + 256] = value
-
-
-def linear_kernel(cot_ref, weight_ref, linear_ref, mix_ref):
+def weight_terms_in(modes_ref, repeat_ref, part, emit):
+    square = (repeat_ref.shape[1] - 256) // 2
+    rows = modes_ref[part]
+    shape = rows.shape[:2] + (256,)
+    high, low = split(rows.reshape(shape[0] * shape[1], 128))
+    side = jnp.concatenate([high, low], axis=1)
+
+    def repeated(start):
+        table = repeat_ref[:, start : start + 256]
+        return dot(side, jnp.concatenate([table, table], axis=0))
+
+    cots = repeated(2 * square)
+    c_real = jnp.concatenate([cots[:, :128]] * 2, axis=1)
+    c_imag = jnp.concatenate([cots[:, 128:]] * 2, axis=1)
+    for start in range(0, square, 256):
+        f_real, f_imag = repeated(start), repeated(square + start)
+        emit(start, (f_real * c_real + f_imag * c_imag).reshape(shape))
+        emit(square + start, (f_real * c_imag - f_imag * c_real).reshape(shape))
+
+
+def weight_kernel(modes_ref, repeat_ref, before_ref, out_hbm, out_ref, sems):
+    pairs = modes_ref.shape[0]
+    copies = []
+    for first in range(0, pairs, pairs // 4):
+        part = pl.ds(first, pairs // 4)
+
+        def emit(start, value):
+            out_ref[part, :, start : start + 256] = before_ref[part, :, start : start + 256] + value
+
+        weight_terms_in(modes_ref, repeat_ref, part, emit)
+        copies.append(pltpu.make_async_copy(out_ref.at[part], out_hbm.at[part], sems.at[len(copies)]))
+        copies[-1].start()
+    for copy in copies:
+        copy.wait()
+
+
+def local_kernel(kept, *refs):
+    cot_hbm, weight_ref = refs[:2]
+    linear_ref, cot_ref, mix_ref, sem = refs[kept + 2], *refs[-3:]
+    copy = pltpu.make_async_copy(cot_hbm, cot_ref, sem)
+    copy.start()
+    if kept:
+        modes_ref, repeat_ref, out_ref = refs[2], refs[3], refs[5]
+        pairs = modes_ref.shape[0]
+        for first in range(0, pairs, pairs // 4):
+            part = pl.ds(first, pairs // 4)
+
+            def emit(start, value):
+                out_ref[part, :, start : start + 256] = value
+
+            weight_terms_in(modes_ref, repeat_ref, part, emit)
     channels, length_y, length_z = cot_ref.shape
     size = 16 * channels
     left = lax.broadcasted_iota(jnp.int32, (size, channels), 0) // 16 == lax.broadcasted_iota(
@@ -300,6 +344,7 @@
         jnp.int32, (size, size), 1
     ) % 16
     mix_ref[...] = jnp.where(same, wide, 0.0).astype(BF16)
+    copy.wait()
     for step in range(length_y // 32):
         columns = []
         for part in range(2):
@@ -313,7 +358,7 @@
             )
 
 
-def inverse_kernel(planes_ref, linear_ref, iz_ref, iy_ref, out_ref, rows_ref):
+def inverse_kernel(planes_ref, linear_ref, iz_ref, iy_ref, out_hbm, rows_ref, out_ref, sems):
     channels, _, length_z = linear_ref.shape
     rows = planes_ref.shape[0]
     pack = 2 * M * M // rows
@@ -383,6 +428,7 @@
     put(along_z(first_half, 0, [0])[:, :length_z], 0, M)
     put(-along_z(first_half, 1, [0])[:, :length_z], 1, M)
     rows_ref[(2 * M + 2) * channels :, :] = jnp.zeros(((ROWS - 2 * M - 2) * channels, length_z), F32)
+    copies = []
     for pair in range(channels // 2):
         columns = [rows_ref[pl.ds(2 * pair + side, ROWS, stride=channels), :] for side in range(2)]
         high, low = split(jnp.concatenate(columns, axis=1))
@@ -391,10 +437,19 @@
             channel = 2 * pair + side
             spectral = value[:, side * length_z : (side + 1) * length_z]
             out_ref[channel] = (spectral + linear_ref[channel]).astype(BF16)
-
-
-def call(kernel, out_shape, scratch, limit, flops, moved, *args, in_specs=None):
-    kwargs = {} if in_specs is None else {"in_specs": in_specs}
+        if pair % 4 == 3:
+            part = pl.ds(2 * pair - 6, 8)
+            copies.append(pltpu.make_async_copy(out_ref.at[part], out_hbm.at[part], sems.at[len(copies)]))
+            copies[-1].start()
+    for copy in copies:
+        copy.wait()
+
+
+def in_hbm(value):
+    return pltpu.with_memory_space_constraint(value, pltpu.HBM)
+
+
+def call(kernel, out_shape, scratch, limit, flops, moved, *args, **kwargs):
     return pl.pallas_call(
         kernel,
         out_shape=out_shape,
@@ -436,9 +491,10 @@
     scale = np.where(np.arange(M) == 0, 1.0, 2.0) / cells
     scale = np.tile(scale, 8).astype(np.float32)[None]
 
+    hbm = pl.BlockSpec(memory_space=pltpu.HBM)
     spectra = call(
         forward_kernel,
-        shape((all_pairs, 128), F32),
+        pltpu.VMEM((all_pairs, 128), F32),
         [
             pltpu.VMEM((2,) + field.shape, BF16),
             pltpu.VMEM(scale.shape, F32),
@@ -447,9 +503,12 @@
             pltpu.VMEM((2 * channels * ROWS, length_z), F32),
             pltpu.SemaphoreType.DMA((7,)),
         ],
-        58, 10**9, 5 * 10**6,
-        field, cotangent, scale, fy, fz,
-        in_specs=[pl.BlockSpec(memory_space=pltpu.HBM)] * 5,
+        16, 10**9, 5 * 10**6,
+        *[in_hbm(one) for one in (field, cotangent, scale, fy, fz)],
+        in_specs=[hbm] * 5,
+    )
+    spectra, spectral_weight, spread, gather = lax.optimization_barrier(
+        (spectra, spectral_weight, spread_table(channels), gather_table(channels))
     )
     received = lax.all_to_all(
         spectra.reshape(groups, pairs, 128), "gx", split_axis=0, concat_axis=0, tiled=True
@@ -457,58 +516,63 @@
     mine, other, grads = call(
         functools.partial(mid_kernel, samples),
         (
-            shape((pairs, share, 128), F32),
-            shape((pairs * (samples - 1), share, 128), F32),
-            shape((width_x * count, 128), F32),
+            pltpu.VMEM((pairs, share, 128), F32),
+            pltpu.VMEM((pairs * (samples - 1), share, 128), F32),
+            pltpu.VMEM((width_x * count, 128), F32),
         ),
         [
             pltpu.VMEM((pairs * kept_x, 128), F32),
-            pltpu.VMEM((pairs * kept_x, 2 * channels * channels), BF16),
-            pltpu.VMEM((pairs * kept_x, 2 * channels * channels), BF16),
+            pltpu.VMEM((2 * pairs * kept_x, channels * channels), BF16),
         ],
         16, 10**9, 4 * 10**6,
-        received.reshape(width_x * pairs, 128), spectral_weight, fx, ix,
-        spread_table(channels), gather_table(channels),
-    )
-    grads, late_cotangent = lax.optimization_barrier((grads, cotangent))
-    linear = call(
-        linear_kernel,
-        shape((channels, length_y, length_z), F32),
-        [pltpu.VMEM((16 * channels, 16 * channels), BF16)],
-        16, 2 * 10**9, 3 * 10**6,
-        late_cotangent, pointwise_weight,
+        received.reshape(width_x * pairs, 128), spectral_weight, fx, ix, spread, gather,
     )
     returned = lax.all_to_all(
         grads.reshape(groups, count, 128), "gx", split_axis=0, concat_axis=0, tiled=True
     )
-    repeat = repeat_table(channels)
-    if samples == 2 and share % 8 == 0:
+    split_samples = samples == 2 and share % 8 == 0
+    kept = [mine, repeat_table(channels)] if split_samples else []
+    tall = (pairs, share, 2 * channels * channels)
+    _, late = lax.optimization_barrier((grads, cotangent))
+    linear, *weight_grad = call(
+        functools.partial(local_kernel, len(kept)),
+        [shape((channels, length_y, length_z), F32)] + [shape(tall, F32)] * (len(kept) // 2),
+        [
+            pltpu.VMEM((channels, length_y, length_z), BF16),
+            pltpu.VMEM((16 * channels, 16 * channels), BF16),
+            pltpu.SemaphoreType.DMA(()),
+        ],
+        16, 4 * 10**9, 5 * 10**6,
+        in_hbm(late), pointwise_weight, *kept,
+        in_specs=[hbm] + [pl.BlockSpec()] * (1 + len(kept)),
+    )
+    if split_samples:
         other = lax.ppermute(other, "dp", [(0, 1), (1, 0)])
-        weight_grad = []
-        for modes in (mine, other):
-            weight_grad = [
-                call(
-                    weight_kernel,
-                    shape((pairs, share, 2 * channels * channels), F32),
-                    [],
-                    16, 2 * 10**9, 3 * 10**6,
-                    modes, repeat, *weight_grad,
-                )
-            ]
-        weight_grad = weight_grad[0]
+        weight_grad = call(
+            weight_kernel,
+            shape(tall, F32),
+            [pltpu.VMEM(tall, F32), pltpu.SemaphoreType.DMA((4,))],
+            16, 2 * 10**9, 5 * 10**6,
+            other, kept[1], *weight_grad,
+            out_specs=hbm,
+        )
     else:
         me = lax.axis_index("dp")
         modes = jnp.concatenate([mine[None], other.reshape(samples - 1, pairs, share, 128)])
         modes = jnp.roll(modes, me, 0)
         modes = lax.all_to_all(modes, "dp", split_axis=0, concat_axis=0, tiled=True)
         weight_grad = weight_terms(modes, channels)
-
     field_grad = call(
         inverse_kernel,
         shape((channels, length_y, length_z), BF16),
-        [pltpu.VMEM((ROWS * channels, length_z), F32)],
+        [
+            pltpu.VMEM((ROWS * channels, length_z), F32),
+            pltpu.VMEM((channels, length_y, length_z), BF16),
+            pltpu.SemaphoreType.DMA((channels // 8,)),
+        ],
         16, 10**9, 4 * 10**6,
         returned.reshape(width_x * count, 128), linear, iz, iy,
+        out_specs=hbm,
     )
     return field_grad.reshape(1, planes, channels, length_y, length_z), weight_grad
 

time: 40.1 us -> 37.9 us (0.945)
  Pallas kernels: 14.7 us -> 13 us
  local copies, waits for them, and re-layouts: 1.4 us -> 0.04 us
  waiting for transfers between devices: 0.45 us -> 1.54 us
    pallas_call x6 -> x5, Pallas kernels: 14.7 us -> 13 us  [call(): pl.pallas_call(kernel, out_shape=out_shape, **kwargs, scratch_shapes=scra...]
    unnamed x18 -> x16, local copies, waits for them, and re-layouts: 1.4 us -> 0.04 us
    ppermute x1, waiting for transfers between devices: 0.45 us -> 1.16 us  [on_device(): other = lax.ppermute(other, 'dp', [(0, 1), (1, 0)])]
  transfers between devices with their start and end apart: 2 -> 2, of which waited for: 1 -> 2; matrix products, arithmetic and copies ran while one was open for 0% -> 0% of each run, Pallas kernels for 13% -> 13%
where the time goes in v3:
time: 37.9 us; the launch traced here: 37.6 us
  blocking collectives  17.2 us (45%)
  Pallas kernels  13 us (34%)
  starting transfers between devices  5.07 us (13%)
  waiting for transfers between devices  1.54 us (4%)
  between operations  0.72 us (2%)
    all_to_all x1, blocking collectives, on_device(): lax.all_to_all(spectra.reshape(groups, pairs, 128), 'gx', split_axis=0, c...  17.2 us
    pallas_call x5, Pallas kernels, call(): pl.pallas_call(kernel, out_shape=out_shape, **kwargs, scratch_shapes=scra...  13 us
    all_to_all x1, starting transfers between devices, on_device(): lax.all_to_all(grads.reshape(groups, count, 128), 'gx', split_axis=0, con...  3.51 us
    ppermute x1, starting transfers between devices, on_device(): other = lax.ppermute(other, 'dp', [(0, 1), (1, 0)])  1.55 us
    ppermute x1, waiting for transfers between devices, on_device(): other = lax.ppermute(other, 'dp', [(0, 1), (1, 0)])  1.16 us
  transfers between devices with their start and end apart: 2, of which 2 were waited for; matrix products, arithmetic and copies ran while one was open for 0% of the time, Pallas kernels for 13%

profile of v3, /device:TPU:0, one launch (start us, length us, event | category | flops | bytes accessed | tf_op | source)
XLA Modules:
  0.0 37.6 jit_solution(16226568191772978037)
XLA Ops:
  0.6 0.0 copy-start.2
  0.6 0.0 copy-start.5
  0.7 0.0 copy-start.6
  0.7 0.0 copy-start.7
  0.7 3.3 %shard_map.149 = f32[512,128]{1,0:T(8,128)S(1)} custom-call(bf16[32,128,128]{2,1,0:T(8,128)(2,1)} %bitcast.11, bf16[32,128,128]{2,1,0:T(8,128)(2,1)} %bitcast.12, f32[1,128]{1,0:T(1,128)} %constant.18.clone.scale_hbm, bf16[48,256]{1,0:T(8,128)(2,1)} %constant.19.clone.fy_hbm, bf16[2,128,256]{2,1,0:T(8,128)(2,1)} %constant.20.clone.fz_hbm), custom_call_target="tpu_custom_call" | custom-call | flops 1000000000 | bytes 5000000 | tf_op jit(solution)/shard_map/pallas_call | solution.py:453
  4.0 17.2 %all_to_all.10 = f32[16,32,128]{2,1,0:T(8,128)S(1)} all-to-all(f32[16,32,128]{2,1,0:T(8,128)S(1)} %bitcast.9), channel_id=1, replica_groups=mesh['dp'=2,'gx'=16] {'gx'}, dimensions={0} | all-to-all | bytes 524288 | tf_op jit(solution)/shard_map/all_to_all | solution.py:513
  21.2 0.0 copy-start.3
  21.2 0.0 copy-start.4
  21.2 0.0 copy-done.2
  21.2 0.0 copy-done.5
  21.2 0.0 copy-done.6
  21.2 0.0 copy-done.7
  21.2 3.0 %shard_map.150 = (f32[32,8,128]{2,1,0:T(8,128)S(1)}, f32[32,8,128]{2,1,0:T(8,128)S(1)}, f32[256,128]{1,0:T(8,128)}) custom-call(f32[512,128]{1,0:T(8,128)S(1)} %bitcast.8, bf16[32,16,2048]{2,1,0:T(8,128)(2,1)S(1)} %copy-done.2, bf16[16,96]{1,0:T(8,128)(2,1)S(1)} %copy-done.7, bf16[16,96]{1,0:T(8,128)(2,1)S(1)} %copy-done.7, bf16[256,256]{1,0:T(8,128)(2,1)S(1)} %copy-done.6, ...), custom_call_target="tpu_custom_call" | custom-call | flops 1000000000 | bytes 4000000 | tf_op jit(solution)/shard_map/pallas_call | solution.py:453
  24.3 3.5 %all-to-all-start.1 = ((f32[16,16,128]{2,1,0:T(8,128)}), f32[16,16,128]{2,1,0:T(8,128)S(1)}, u32[]{:S(2)}, u32[]{:S(2)}) async-start(f32[16,16,128]{2,1,0:T(8,128)} %bitcast.4), calls=%async_computation.1 | async-start | bytes 262144 | tf_op jit(solution)/shard_map/all_to_all | solution.py:530
  27.8 1.6 %collective-permute-start = (f32[32,8,128]{2,1,0:T(8,128)S(1)}, f32[32,8,128]{2,1,0:T(8,128)S(1)}, u32[]{:S(2)}, u32[]{:S(2)}) collective-permute-start(f32[32,8,128]{2,1,0:T(8,128)S(1)} %get-tuple-element.20), channel_id=1, source_target_pairs={{0,16},{16,0},{1,17},{17,1},{2,18},{18,2},{3,19},{19,3},{4,20},{20... | collective-permute-start | bytes 393224 | tf_op jit(solution)/shard_map/ppermute | solution.py:550
  29.3 0.0 copy-done.3
  29.4 0.0 copy-done.4
  29.4 3.0 %shard_map.151 = (f32[32,128,128]{2,1,0:T(8,128)S(1)}, f32[32,8,2048]{2,1,0:T(8,128)S(1)}) custom-call(bf16[32,128,128]{2,1,0:T(8,128)(2,1)} %bitcast.13, bf16[32,32]{1,0:T(8,128)(2,1)S(1)} %copy-done.3, f32[32,8,128]{2,1,0:T(8,128)S(1)} %get-tuple-element.18.refs_2_, bf16[128,2304]{1,0:T(8,128)(2,1)S(1)} %copy-done.4), custom_call_target="tpu_custom_call" | custom-call | flops 4000000000 | bytes 5000000 | tf_op jit(solution)/shard_map/pallas_call | solution.py:453
  32.3 1.2 %collective-permute-done.modes_ref = f32[32,8,128]{2,1,0:T(8,128)S(1)} collective-permute-done((f32[32,8,128]{2,1,0:T(8,128)S(1)}, f32[32,8,128]{2,1,0:T(8,128)S(1)}, u32[]{:S(2)}, u32[]{:S(2)}) %collective-permute-start) | collective-permute-done | bytes 131104 | tf_op jit(solution)/shard_map/ppermute | solution.py:550
  33.5 0.0 copy-start
  33.5 0.0 copy-start.1
  33.5 1.8 %shard_map.153 = f32[32,8,2048]{2,1,0:T(8,128)} custom-call(f32[32,8,128]{2,1,0:T(8,128)S(1)} %collective-permute-done.modes_ref, bf16[128,2304]{1,0:T(8,128)(2,1)S(1)} %copy-done.4, f32[32,8,2048]{2,1,0:T(8,128)S(1)} %get-tuple-element.21.before_ref), custom_call_target="tpu_custom_call" | custom-call | flops 2000000000 | bytes 5000000 | tf_op jit(solution)/shard_map/pallas_call | solution.py:453
  35.3 0.4 all-to-all-done.1
  35.7 0.0 copy-done
  35.7 0.0 copy-done.1
  35.7 1.9 %shard_map.152 = bf16[32,128,128]{2,1,0:T(8,128)(2,1)} custom-call(f32[256,128]{1,0:T(8,128)S(1)} %bitcast.7, f32[32,128,128]{2,1,0:T(8,128)S(1)} %get-tuple-element.19.linear_ref, bf16[2,2,256,256]{3,2,1,0:T(8,128)(2,1)S(1)} %copy-done, bf16[128,144]{1,0:T(8,128)(2,1)S(1)} %copy-done.1), custom_call_target="tpu_custom_call" | custom-call | flops 1000000000 | bytes 4000000 | tf_op jit(solution)/shard_map/pallas_call | solution.py:453
Async XLA Ops:
  0.6 20.6 %copy-start.2 = (bf16[32,16,2048]{2,1,0:T(8,128)(2,1)S(1)}, bf16[32,16,2048]{2,1,0:T(8,128)(2,1)}, u32[]{:S(2)}) copy-start(bf16[32,16,2048]{2,1,0:T(8,128)(2,1)} %weight_ref) | copy-start | bytes 6291460
  0.6 20.6 %copy-start.5 = (bf16[1024,256]{1,0:T(8,128)(2,1)S(1)}, bf16[1024,256]{1,0:T(8,128)(2,1)}, u32[]{:S(2)}) copy-start(bf16[1024,256]{1,0:T(8,128)(2,1)} %constant.22.clone.gather_ref) | copy-start | bytes 1572868
  0.7 20.6 %copy-start.6 = (bf16[256,256]{1,0:T(8,128)(2,1)S(1)}, bf16[256,256]{1,0:T(8,128)(2,1)}, u32[]{:S(2)}) copy-start(bf16[256,256]{1,0:T(8,128)(2,1)} %constant.21.clone.spread_ref) | copy-start | bytes 393220
  0.7 20.6 %copy-start.7 = (bf16[16,96]{1,0:T(8,128)(2,1)S(1)}, bf16[16,96]{1,0:T(8,128)(2,1)}, u32[]{:S(2)}) copy-start(bf16[16,96]{1,0:T(8,128)(2,1)} %constant.23.clone.fx_ref.ix_ref) | copy-start | bytes 9220
  21.2 8.1 %copy-start.3 = (bf16[32,32]{1,0:T(8,128)(2,1)S(1)}, bf16[32,32]{1,0:T(8,128)(2,1)}, u32[]{:S(2)}) copy-start(bf16[32,32]{1,0:T(8,128)(2,1)} %refs_1_.1) | copy-start | bytes 6148
  21.2 8.1 %copy-start.4 = (bf16[128,2304]{1,0:T(8,128)(2,1)S(1)}, bf16[128,2304]{1,0:T(8,128)(2,1)}, u32[]{:S(2)}) copy-start(bf16[128,2304]{1,0:T(8,128)(2,1)} %constant.24.clone.refs_3_.repeat_ref) | copy-start | bytes 1769476
  24.3 11.4 %all-to-all-start.1 = ((f32[16,16,128]{2,1,0:T(8,128)}), f32[16,16,128]{2,1,0:T(8,128)S(1)}, u32[]{:S(2)}, u32[]{:S(2)}) async-start(f32[16,16,128]{2,1,0:T(8,128)} %bitcast.4), calls=%async_computation.1 | async-start | bytes 262144 | tf_op jit(solution)/shard_map/all_to_all | solution.py:530
  27.8 5.7 %collective-permute-start = (f32[32,8,128]{2,1,0:T(8,128)S(1)}, f32[32,8,128]{2,1,0:T(8,128)S(1)}, u32[]{:S(2)}, u32[]{:S(2)}) collective-permute-start(f32[32,8,128]{2,1,0:T(8,128)S(1)} %get-tuple-element.20), channel_id=1, source_target_pairs={{0,16},{16,0},{1,17},{17,1},{2,18},{18,2},{3,19},{19,3},{4,20},{20... | collective-permute-start | bytes 393224 | tf_op jit(solution)/shard_map/ppermute | solution.py:550
  33.5 2.2 %copy-start = (bf16[2,2,256,256]{3,2,1,0:T(8,128)(2,1)S(1)}, bf16[2,2,256,256]{3,2,1,0:T(8,128)(2,1)}, u32[]{:S(2)}) copy-start(bf16[2,2,256,256]{3,2,1,0:T(8,128)(2,1)} %constant.25.clone.iz_ref) | copy-start | bytes 1572868
  33.5 2.2 %copy-start.1 = (bf16[128,144]{1,0:T(8,128)(2,1)S(1)}, bf16[128,144]{1,0:T(8,128)(2,1)}, u32[]{:S(2)}) copy-start(bf16[128,144]{1,0:T(8,128)(2,1)} %constant.26.clone.iy_ref) | copy-start | bytes 110596

commit v4 on v3

--- a/solution.py
+++ b/solution.py
@@ -15,6 +15,7 @@
 BF16 = jnp.bfloat16
 MIB = 1024 * 1024
 ROWS = 3 * M
+PITCH = ROWS - 8
 
 
 def kept_freqs(half_count, length):
@@ -49,7 +50,7 @@
     rows = np.zeros((ROWS, length_y))
     rows[:M], rows[M : 2 * M] = cos_y[:M], -sin_y[:M]
     rows[2 * M], rows[2 * M + 1] = cos_y[M], -sin_y[M]
-    along_y = np.concatenate(split_np(rows), 1)
+    along_y = np.concatenate(split_np(rows), 0)
     cos_z, sin_z = phases(np.arange(M), length_z)
     along_z = np.concatenate([np.tile(cos_z.T, (1, 8)), np.tile(sin_z.T, (1, 8))], 1)
     return along_y, np.stack(split_np(along_z))
@@ -96,17 +97,22 @@
     return table.reshape(8 * channels, 256).astype(ml_dtypes.bfloat16)
 
 
+LEVELS = 1
+
+
 def gather_table(channels):
-    square = channels * channels
-    table = np.zeros((2, square // 256, 128, 2, 2, 2, channels))
-    for pair in range(square // 256):
-        for lane in range(128):
-            i = (pair * 256 + (lane % 32 >= 16) * 128 + lane) // channels
-            table[0, pair, lane, 0, :, 0, i] = 1.0
-            table[1, pair, lane, 0, :, 1, i] = 1.0
-            table[1, pair, lane, 1, :, 0, i] = -1.0
-            table[0, pair, lane, 1, :, 1, i] = 1.0
-    return table.reshape(square, 8 * channels).astype(ml_dtypes.bfloat16)
+    width = channels * channels >> LEVELS
+    place = np.arange(width)
+    block, lane = place // 128, place % 128
+    step = block << LEVELS
+    for level in range(LEVELS):
+        step = step + ((lane & 16 >> level) > 0) * (1 << level)
+    i = step * (128 // channels) + lane // channels
+    table = np.zeros((2, width, 2, 2, 2, channels))
+    for part in range(2):
+        table[part, place, 0, :, part, i] = 1.0
+        table[part, place, 1, :, 1 - part, i] = 1.0 - 2.0 * part
+    return table.reshape(2 * width, 8 * channels).astype(ml_dtypes.bfloat16)
 
 
 def repeat_table(channels):
@@ -122,7 +128,7 @@
 
 def forward_kernel(
     field_hbm, cot_hbm, scale_hbm, fy_hbm, fz_hbm,
-    out_ref, data_ref, scale_ref, fy_ref, fz_ref, rows_ref, sems,
+    out_ref, data_ref, scale_ref, fy_ref, fz_ref, spread_ref, rows_ref, sems,
 ):
     channels, _, length_z = field_hbm.shape
     copies = []
@@ -134,37 +140,40 @@
         return copy
 
     half = channels // 2
+    table_z = start(fz_hbm, fz_ref)
     table_y = start(fy_hbm, fy_ref)
     chunks = []
     for array, ref in enumerate((field_hbm, cot_hbm)):
         for first in (0, half):
             part = pl.ds(first, half)
             chunks.append((array, first, start(ref.at[part], data_ref.at[array, part])))
-        if array == 0:
-            table_z = start(fz_hbm, fz_ref)
-            table_scale = start(scale_hbm, scale_ref)
+    table_scale = start(scale_hbm, scale_ref)
+    table_z.wait()
+    group = lax.broadcasted_iota(jnp.int32, (16, 256), 1) // M % 8
+    for place in range(8):
+        keep = jnp.where(group == place, 1.0, 0.0).astype(BF16)
+        keep = jnp.concatenate([keep] * (length_z // 16), axis=0)
+        for term in range(2):
+            spread_ref[place, term * length_z : (term + 1) * length_z, :] = fz_ref[term] * keep
     table_y.wait()
     for array, first, copy in chunks:
         copy.wait()
         for pair in range(first // 2, (first + half) // 2):
             data = jnp.concatenate([data_ref[array, 2 * pair], data_ref[array, 2 * pair + 1]], axis=1)
-            value = dot(fy_ref[...], jnp.concatenate([data, data], axis=0))
-            base = (array * channels + 2 * pair) * ROWS
-            rows_ref[base : base + ROWS, :] = value[:, :length_z]
-            rows_ref[base + ROWS : base + 2 * ROWS, :] = value[:, length_z:]
-    table_z.wait()
+            both = dot(fy_ref[...], data)
+            value = both[:PITCH] + both[ROWS : ROWS + PITCH]
+            base = (array * channels + 2 * pair) * PITCH
+            rows_ref[base : base + PITCH, :] = value[:, :length_z]
+            rows_ref[base + PITCH : base + 2 * PITCH, :] = value[:, length_z:]
     table_scale.wait()
     count = 2 * channels
-    group = lax.broadcasted_iota(jnp.int32, (16, 256), 1) // M % 8
     lefts, rights = [], []
     for place in range(8):
-        keep = jnp.where(group == place, 1.0, 0.0).astype(BF16)
-        keep = jnp.concatenate([keep] * (length_z // 16), axis=0)
-        table_high, table_low = fz_ref[0] * keep, fz_ref[1] * keep
+        table_high, table_low = spread_ref[place, :length_z], spread_ref[place, length_z:]
         sources = [part * M + octet * 8 + place for part in range(2) for octet in range(2)]
         if place == 0:
             sources += [2 * M, 2 * M + 1]
-        rows = [rows_ref[pl.ds(source, count, stride=ROWS), :] for source in sources]
+        rows = [rows_ref[pl.ds(source, count, stride=PITCH), :] for source in sources]
         high, low = split(jnp.concatenate(rows, axis=0))
         left = jnp.concatenate([high, low, high], axis=1)
         right = jnp.concatenate([table_high, table_high, table_low], axis=0)
@@ -228,13 +237,14 @@
                     other_ref[(ahead - 1) * pairs + q] = part
 
     square = weight_ref.shape[2] // 2
-    lane = lax.broadcasted_iota(jnp.int32, (kept_x, 128), 1) % 32
-    first_half = lane < 16
-
-    def halved(one, two):
-        kept = jnp.where(first_half, one, two)
-        moved = jnp.where(first_half, two, one)
-        return kept + jnp.where(first_half, pltpu.roll(moved, 112, 1), pltpu.roll(moved, 16, 1))
+    width = square >> LEVELS
+    lane = lax.broadcasted_iota(jnp.int32, (kept_x, 128), 1)
+
+    def merge(one, two, shift):
+        first = lane & shift == 0
+        moved = jnp.where(first, two, one)
+        moved = jnp.take_along_axis(moved, lane ^ shift, axis=1, mode="promise_in_bounds")
+        return jnp.where(first, one, two) + moved
 
     def products(rows, q, start):
         real, imag = rows[:, :128], rows[:, 128:]
@@ -252,14 +262,19 @@
         for place in range(chunk):
             rows = spread[place * kept_x : (place + 1) * kept_x]
             at = base + place * kept_x
-            for start in range(0, square, 256):
-                ones = products(rows, first + place, start)
-                twos = products(rows, first + place, start + 128)
+            for column in range(0, width, 128):
+                items = [
+                    products(rows, first + place, start)
+                    for start in range(column << LEVELS, column + 128 << LEVELS, 128)
+                ]
                 for part in range(2):
-                    column = (part * square + start) // 2
-                    high, low = split(halved(ones[part], twos[part]))
-                    split_ref[at : at + kept_x, column : column + 128] = high
-                    split_ref[at + size : at + size + kept_x, column : column + 128] = low
+                    values = [item[part] for item in items]
+                    for level in range(LEVELS):
+                        values = [merge(one, two, 16 >> level) for one, two in zip(values[::2], values[1::2])]
+                    high, low = split(values[0])
+                    at_column = part * width + column
+                    split_ref[at : at + kept_x, at_column : at_column + 128] = high
+                    split_ref[at + size : at + size + kept_x, at_column : at_column + 128] = low
         both = dot(split_ref[base : base + 2 * size, :], gather_ref[...])
         grads.append(both[:size] + both[size:])
     grads = jnp.concatenate(grads, axis=0)
@@ -361,6 +376,7 @@
 def inverse_kernel(planes_ref, linear_ref, iz_ref, iy_ref, out_hbm, rows_ref, out_ref, sems):
     channels, _, length_z = linear_ref.shape
     rows = planes_ref.shape[0]
+    pitch = channels + 8
     pack = 2 * M * M // rows
     group = lax.broadcasted_iota(jnp.int32, (16, 256), 1) // M % 8
     keeps = []
@@ -394,7 +410,7 @@
         return dot(jnp.concatenate(left, axis=0), right)
 
     def put(value, part, k):
-        first = mode_row(part, k) * channels
+        first = mode_row(part, k) * pitch
         rows_ref[first : first + channels, :] = value
 
     blocks = rows // M
@@ -427,10 +443,10 @@
     first_half = halves(last)[:1]
     put(along_z(first_half, 0, [0])[:, :length_z], 0, M)
     put(-along_z(first_half, 1, [0])[:, :length_z], 1, M)
-    rows_ref[(2 * M + 2) * channels :, :] = jnp.zeros(((ROWS - 2 * M - 2) * channels, length_z), F32)
+    rows_ref[(2 * M + 2) * pitch :, :] = jnp.zeros(((ROWS - 2 * M - 2) * pitch, length_z), F32)
     copies = []
     for pair in range(channels // 2):
-        columns = [rows_ref[pl.ds(2 * pair + side, ROWS, stride=channels), :] for side in range(2)]
+        columns = [rows_ref[pl.ds(2 * pair + side, ROWS, stride=pitch), :] for side in range(2)]
         high, low = split(jnp.concatenate(columns, axis=1))
         value = dot(iy_ref[...], jnp.concatenate([high, low, high], axis=0))
         for side in range(2):
@@ -500,7 +516,8 @@
             pltpu.VMEM(scale.shape, F32),
             pltpu.VMEM(fy.shape, BF16),
             pltpu.VMEM(fz.shape, BF16),
-            pltpu.VMEM((2 * channels * ROWS, length_z), F32),
+            pltpu.VMEM((8, 2 * length_z, 256), BF16),
+            pltpu.VMEM((2 * channels * PITCH, length_z), F32),
             pltpu.SemaphoreType.DMA((7,)),
         ],
         16, 10**9, 5 * 10**6,
@@ -522,7 +539,7 @@
         ),
         [
             pltpu.VMEM((pairs * kept_x, 128), F32),
-            pltpu.VMEM((2 * pairs * kept_x, channels * channels), BF16),
+            pltpu.VMEM((2 * pairs * kept_x, gather.shape[0]), BF16),
         ],
         16, 10**9, 4 * 10**6,
         received.reshape(width_x * pairs, 128), spectral_weight, fx, ix, spread, gather,
@@ -566,7 +583,7 @@
         inverse_kernel,
         shape((channels, length_y, length_z), BF16),
         [
-            pltpu.VMEM((ROWS * channels, length_z), F32),
+            pltpu.VMEM((ROWS * (channels + 8), length_z), F32),
             pltpu.VMEM((channels, length_y, length_z), BF16),
             pltpu.SemaphoreType.DMA((channels // 8,)),
         ],

time: 37.9 us -> 37.4 us (0.987)
  Pallas kernels: 13 us -> 12.5 us
    pallas_call x5, Pallas kernels: 13 us -> 12.5 us  [call(): pl.pallas_call(kernel, out_shape=out_shape, **kwargs, scratch_shapes=scra...]
where the time goes in v4:
time: 37.4 us; the launch traced here: 37.1 us
  blocking collectives  17.2 us (46%)
  Pallas kernels  12.5 us (33%)
  starting transfers between devices  5.06 us (14%)
  waiting for transfers between devices  1.54 us (4%)
  between operations  0.72 us (2%)
    all_to_all x1, blocking collectives, on_device(): lax.all_to_all(spectra.reshape(groups, pairs, 128), 'gx', split_axis=0, c...  17.2 us
    pallas_call x5, Pallas kernels, call(): pl.pallas_call(kernel, out_shape=out_shape, **kwargs, scratch_shapes=scra...  12.5 us
    all_to_all x1, starting transfers between devices, on_device(): lax.all_to_all(grads.reshape(groups, count, 128), 'gx', split_axis=0, con...  3.51 us
    ppermute x1, starting transfers between devices, on_device(): other = lax.ppermute(other, 'dp', [(0, 1), (1, 0)])  1.55 us
    ppermute x1, waiting for transfers between devices, on_device(): other = lax.ppermute(other, 'dp', [(0, 1), (1, 0)])  1.17 us
  transfers between devices with their start and end apart: 2, of which 2 were waited for; matrix products, arithmetic and copies ran while one was open for 0% of the time, Pallas kernels for 13%

profile of v4, /device:TPU:0, one launch (start us, length us, event | category | flops | bytes accessed | tf_op | source)
XLA Modules:
  0.0 37.1 jit_solution(8022369392940851241)
XLA Ops:
  0.6 0.0 copy-start.2
  0.6 0.0 copy-start.5
  0.7 0.0 copy-start.6
  0.7 0.0 copy-start.7
  0.7 3.1 %shard_map.149 = f32[512,128]{1,0:T(8,128)S(1)} custom-call(bf16[32,128,128]{2,1,0:T(8,128)(2,1)} %bitcast.11, bf16[32,128,128]{2,1,0:T(8,128)(2,1)} %bitcast.12, f32[1,128]{1,0:T(1,128)} %constant.18.clone.scale_hbm, bf16[96,128]{1,0:T(8,128)(2,1)} %constant.19.clone.fy_hbm, bf16[2,128,256]{2,1,0:T(8,128)(2,1)} %constant.20.clone.fz_hbm), custom_call_target="tpu_custom_call" | custom-call | flops 1000000000 | bytes 5000000 | tf_op jit(solution)/shard_map/pallas_call | solution.py:469
  3.8 17.2 %all_to_all.10 = f32[16,32,128]{2,1,0:T(8,128)S(1)} all-to-all(f32[16,32,128]{2,1,0:T(8,128)S(1)} %bitcast.9), channel_id=1, replica_groups=mesh['dp'=2,'gx'=16] {'gx'}, dimensions={0} | all-to-all | bytes 524288 | tf_op jit(solution)/shard_map/all_to_all | solution.py:530
  21.0 0.0 copy-start.3
  21.0 0.0 copy-start.4
  21.0 0.0 copy-done.2
  21.0 0.0 copy-done.5
  21.0 0.0 copy-done.6
  21.0 0.0 copy-done.7
  21.1 2.9 %shard_map.150 = (f32[32,8,128]{2,1,0:T(8,128)S(1)}, f32[32,8,128]{2,1,0:T(8,128)S(1)}, f32[256,128]{1,0:T(8,128)}) custom-call(f32[512,128]{1,0:T(8,128)S(1)} %bitcast.8, bf16[32,16,2048]{2,1,0:T(8,128)(2,1)S(1)} %copy-done.2, bf16[16,96]{1,0:T(8,128)(2,1)S(1)} %copy-done.7, bf16[16,96]{1,0:T(8,128)(2,1)S(1)} %copy-done.7, bf16[256,256]{1,0:T(8,128)(2,1)S(1)} %copy-done.6, ...), custom_call_target="tpu_custom_call" | custom-call | flops 1000000000 | bytes 4000000 | tf_op jit(solution)/shard_map/pallas_call | solution.py:469
  24.0 3.5 %all-to-all-start.1 = ((f32[16,16,128]{2,1,0:T(8,128)}), f32[16,16,128]{2,1,0:T(8,128)S(1)}, u32[]{:S(2)}, u32[]{:S(2)}) async-start(f32[16,16,128]{2,1,0:T(8,128)} %bitcast.4), calls=%async_computation.1 | async-start | bytes 262144 | tf_op jit(solution)/shard_map/all_to_all | solution.py:547
  27.5 1.5 %collective-permute-start = (f32[32,8,128]{2,1,0:T(8,128)S(1)}, f32[32,8,128]{2,1,0:T(8,128)S(1)}, u32[]{:S(2)}, u32[]{:S(2)}) collective-permute-start(f32[32,8,128]{2,1,0:T(8,128)S(1)} %get-tuple-element.20), channel_id=1, source_target_pairs={{0,16},{16,0},{1,17},{17,1},{2,18},{18,2},{3,19},{19,3},{4,20},{20... | collective-permute-start | bytes 393224 | tf_op jit(solution)/shard_map/ppermute | solution.py:567
  29.0 0.0 copy-done.3
  29.0 0.0 copy-done.4
  29.0 3.0 %shard_map.151 = (f32[32,128,128]{2,1,0:T(8,128)S(1)}, f32[32,8,2048]{2,1,0:T(8,128)S(1)}) custom-call(bf16[32,128,128]{2,1,0:T(8,128)(2,1)} %bitcast.13, bf16[32,32]{1,0:T(8,128)(2,1)S(1)} %copy-done.3, f32[32,8,128]{2,1,0:T(8,128)S(1)} %get-tuple-element.18.refs_2_, bf16[128,2304]{1,0:T(8,128)(2,1)S(1)} %copy-done.4), custom_call_target="tpu_custom_call" | custom-call | flops 4000000000 | bytes 5000000 | tf_op jit(solution)/shard_map/pallas_call | solution.py:469
  32.0 1.2 %collective-permute-done.modes_ref = f32[32,8,128]{2,1,0:T(8,128)S(1)} collective-permute-done((f32[32,8,128]{2,1,0:T(8,128)S(1)}, f32[32,8,128]{2,1,0:T(8,128)S(1)}, u32[]{:S(2)}, u32[]{:S(2)}) %collective-permute-start) | collective-permute-done | bytes 131104 | tf_op jit(solution)/shard_map/ppermute | solution.py:567
  33.2 0.0 copy-start
  33.2 0.0 copy-start.1
  33.2 1.8 %shard_map.153 = f32[32,8,2048]{2,1,0:T(8,128)} custom-call(f32[32,8,128]{2,1,0:T(8,128)S(1)} %collective-permute-done.modes_ref, bf16[128,2304]{1,0:T(8,128)(2,1)S(1)} %copy-done.4, f32[32,8,2048]{2,1,0:T(8,128)S(1)} %get-tuple-element.21.before_ref), custom_call_target="tpu_custom_call" | custom-call | flops 2000000000 | bytes 5000000 | tf_op jit(solution)/shard_map/pallas_call | solution.py:469
  35.0 0.4 %all-to-all-done.1 = f32[16,16,128]{2,1,0:T(8,128)S(1)} async-done(((f32[16,16,128]{2,1,0:T(8,128)}), f32[16,16,128]{2,1,0:T(8,128)S(1)}, u32[]{:S(2)}, u32[]{:S(2)}) %all-to-all-start.1) | async-done | bytes 131104 | tf_op jit(solution)/shard_map/all_to_all | solution.py:547
  35.4 0.0 copy-done
  35.4 0.0 copy-done.1
  35.4 1.8 %shard_map.152 = bf16[32,128,128]{2,1,0:T(8,128)(2,1)} custom-call(f32[256,128]{1,0:T(8,128)S(1)} %bitcast.7, f32[32,128,128]{2,1,0:T(8,128)S(1)} %get-tuple-element.19.linear_ref, bf16[2,2,256,256]{3,2,1,0:T(8,128)(2,1)S(1)} %copy-done, bf16[128,144]{1,0:T(8,128)(2,1)S(1)} %copy-done.1), custom_call_target="tpu_custom_call" | custom-call | flops 1000000000 | bytes 4000000 | tf_op jit(solution)/shard_map/pallas_call | solution.py:469
Async XLA Ops:
  0.6 20.4 %copy-start.2 = (bf16[32,16,2048]{2,1,0:T(8,128)(2,1)S(1)}, bf16[32,16,2048]{2,1,0:T(8,128)(2,1)}, u32[]{:S(2)}) copy-start(bf16[32,16,2048]{2,1,0:T(8,128)(2,1)} %weight_ref) | copy-start | bytes 6291460
  0.6 20.4 %copy-start.5 = (bf16[1024,256]{1,0:T(8,128)(2,1)S(1)}, bf16[1024,256]{1,0:T(8,128)(2,1)}, u32[]{:S(2)}) copy-start(bf16[1024,256]{1,0:T(8,128)(2,1)} %constant.22.clone.gather_ref) | copy-start | bytes 1572868
  0.7 20.4 %copy-start.6 = (bf16[256,256]{1,0:T(8,128)(2,1)S(1)}, bf16[256,256]{1,0:T(8,128)(2,1)}, u32[]{:S(2)}) copy-start(bf16[256,256]{1,0:T(8,128)(2,1)} %constant.21.clone.spread_ref) | copy-start | bytes 393220
  0.7 20.4 %copy-start.7 = (bf16[16,96]{1,0:T(8,128)(2,1)S(1)}, bf16[16,96]{1,0:T(8,128)(2,1)}, u32[]{:S(2)}) copy-start(bf16[16,96]{1,0:T(8,128)(2,1)} %constant.23.clone.fx_ref.ix_ref) | copy-start | bytes 9220
  21.0 8.0 %copy-start.3 = (bf16[32,32]{1,0:T(8,128)(2,1)S(1)}, bf16[32,32]{1,0:T(8,128)(2,1)}, u32[]{:S(2)}) copy-start(bf16[32,32]{1,0:T(8,128)(2,1)} %refs_1_.1) | copy-start | bytes 6148
  21.0 8.0 %copy-start.4 = (bf16[128,2304]{1,0:T(8,128)(2,1)S(1)}, bf16[128,2304]{1,0:T(8,128)(2,1)}, u32[]{:S(2)}) copy-start(bf16[128,2304]{1,0:T(8,128)(2,1)} %constant.24.clone.refs_3_.repeat_ref) | copy-start | bytes 1769476
  24.0 11.4 %all-to-all-start.1 = ((f32[16,16,128]{2,1,0:T(8,128)}), f32[16,16,128]{2,1,0:T(8,128)S(1)}, u32[]{:S(2)}, u32[]{:S(2)}) async-start(f32[16,16,128]{2,1,0:T(8,128)} %bitcast.4), calls=%async_computation.1 | async-start | bytes 262144 | tf_op jit(solution)/shard_map/all_to_all | solution.py:547
  27.5 5.7 %collective-permute-start = (f32[32,8,128]{2,1,0:T(8,128)S(1)}, f32[32,8,128]{2,1,0:T(8,128)S(1)}, u32[]{:S(2)}, u32[]{:S(2)}) collective-permute-start(f32[32,8,128]{2,1,0:T(8,128)S(1)} %get-tuple-element.20), channel_id=1, source_target_pairs={{0,16},{16,0},{1,17},{17,1},{2,18},{18,2},{3,19},{19,3},{4,20},{20... | collective-permute-start | bytes 393224 | tf_op jit(solution)/shard_map/ppermute | solution.py:567
  33.2 2.2 %copy-start = (bf16[2,2,256,256]{3,2,1,0:T(8,128)(2,1)S(1)}, bf16[2,2,256,256]{3,2,1,0:T(8,128)(2,1)}, u32[]{:S(2)}) copy-start(bf16[2,2,256,256]{3,2,1,0:T(8,128)(2,1)} %constant.25.clone.iz_ref) | copy-start | bytes 1572868
  33.2 2.2 %copy-start.1 = (bf16[128,144]{1,0:T(8,128)(2,1)S(1)}, bf16[128,144]{1,0:T(8,128)(2,1)}, u32[]{:S(2)}) copy-start(bf16[128,144]{1,0:T(8,128)(2,1)} %constant.26.clone.iy_ref) | copy-start | bytes 110596

commit v5 on v4

--- a/solution.py
+++ b/solution.py
@@ -50,10 +50,10 @@
     rows = np.zeros((ROWS, length_y))
     rows[:M], rows[M : 2 * M] = cos_y[:M], -sin_y[:M]
     rows[2 * M], rows[2 * M + 1] = cos_y[M], -sin_y[M]
-    along_y = np.concatenate(split_np(rows), 0)
+    along_y = np.concatenate(split_np(rows), 1)
     cos_z, sin_z = phases(np.arange(M), length_z)
     along_z = np.concatenate([np.tile(cos_z.T, (1, 8)), np.tile(sin_z.T, (1, 8))], 1)
-    return along_y, np.stack(split_np(along_z))
+    return np.concatenate((along_y,) + split_np(along_z))
 
 
 def inverse_tables(length_y, length_z):
@@ -127,10 +127,9 @@
 
 
 def forward_kernel(
-    field_hbm, cot_hbm, scale_hbm, fy_hbm, fz_hbm,
-    out_ref, data_ref, scale_ref, fy_ref, fz_ref, spread_ref, rows_ref, sems,
+    cells, field_hbm, cot_hbm, table_hbm, out_ref, data_ref, table_ref, spread_ref, rows_ref, sems
 ):
-    channels, _, length_z = field_hbm.shape
+    channels, length_y, length_z = field_hbm.shape
     copies = []
 
     def start(source, target):
@@ -139,33 +138,30 @@
         copies.append(copy)
         return copy
 
-    half = channels // 2
-    table_z = start(fz_hbm, fz_ref)
-    table_y = start(fy_hbm, fy_ref)
-    chunks = []
-    for array, ref in enumerate((field_hbm, cot_hbm)):
-        for first in (0, half):
-            part = pl.ds(first, half)
-            chunks.append((array, first, start(ref.at[part], data_ref.at[array, part])))
-    table_scale = start(scale_hbm, scale_ref)
-    table_z.wait()
+    table = start(table_hbm, table_ref)
+    chunks = [start(ref, data_ref.at[array]) for array, ref in enumerate((field_hbm, cot_hbm))]
+    table.wait()
+    along_y = jnp.concatenate([table_ref[:ROWS, :length_y], table_ref[:ROWS, length_y:]], axis=0)
     group = lax.broadcasted_iota(jnp.int32, (16, 256), 1) // M % 8
     for place in range(8):
         keep = jnp.where(group == place, 1.0, 0.0).astype(BF16)
         keep = jnp.concatenate([keep] * (length_z // 16), axis=0)
         for term in range(2):
-            spread_ref[place, term * length_z : (term + 1) * length_z, :] = fz_ref[term] * keep
-    table_y.wait()
-    for array, first, copy in chunks:
+            first = ROWS + term * length_z
+            spread_ref[place, term * length_z : (term + 1) * length_z, :] = (
+                table_ref[first : first + length_z, :] * keep
+            )
+    for array, copy in enumerate(chunks):
         copy.wait()
-        for pair in range(first // 2, (first + half) // 2):
+        for pair in range(channels // 2):
             data = jnp.concatenate([data_ref[array, 2 * pair], data_ref[array, 2 * pair + 1]], axis=1)
-            both = dot(fy_ref[...], data)
+            both = dot(along_y, data)
             value = both[:PITCH] + both[ROWS : ROWS + PITCH]
             base = (array * channels + 2 * pair) * PITCH
             rows_ref[base : base + PITCH, :] = value[:, :length_z]
             rows_ref[base + PITCH : base + 2 * PITCH, :] = value[:, length_z:]
-    table_scale.wait()
+    kz = lax.broadcasted_iota(jnp.int32, (1, 128), 1) % M
+    scale = jnp.where(kz == 0, 1.0 / cells, 2.0 / cells).astype(F32)
     count = 2 * channels
     lefts, rights = [], []
     for place in range(8):
@@ -191,7 +187,7 @@
             block = (real[:, :128] - imag[:, 128:], -imag[:, :128] - real[:, 128:])
         scaled = []
         for part in block:
-            scaled += [part[:channels], part[channels:] * scale_ref[...]]
+            scaled += [part[:channels], part[channels:] * scale]
         return jnp.concatenate(scaled, axis=0).T
 
     for octet in range(2):
@@ -228,13 +224,14 @@
         for index, q in enumerate((2 * step, 2 * step + 1)):
             mode = modes[:, index * 128 : (index + 1) * 128]
             rows_ref[q * kept_x : (q + 1) * kept_x, :] = mode
-            for ahead in range(samples):
-                start = q * kept_x + lax.rem(me + ahead, samples) * share
-                part = rows_ref[pl.ds(pl.multiple_of(start, share), share), :]
-                if ahead == 0:
-                    mine_ref[q] = part
-                else:
-                    other_ref[(ahead - 1) * pairs + q] = part
+    for q in range(pairs):
+        for ahead in range(samples):
+            start = q * kept_x + lax.rem(me + ahead, samples) * share
+            part = rows_ref[pl.ds(pl.multiple_of(start, share), share), :]
+            if ahead == 0:
+                mine_ref[q] = part
+            else:
+                other_ref[(ahead - 1) * pairs + q] = part
 
     square = weight_ref.shape[2] // 2
     width = square >> LEVELS
@@ -501,28 +498,23 @@
     field = field.reshape(channels, length_y, length_z)
     cotangent = cotangent.reshape(channels, length_y, length_z)
 
-    fy, fz = forward_tables(length_y, length_z)
+    forward = forward_tables(length_y, length_z)
     iz, iy = inverse_tables(length_y, length_z)
     fx, ix = x_tables(kept_x, width_x)
-    scale = np.where(np.arange(M) == 0, 1.0, 2.0) / cells
-    scale = np.tile(scale, 8).astype(np.float32)[None]
-
     hbm = pl.BlockSpec(memory_space=pltpu.HBM)
     spectra = call(
-        forward_kernel,
+        functools.partial(forward_kernel, cells),
         pltpu.VMEM((all_pairs, 128), F32),
         [
             pltpu.VMEM((2,) + field.shape, BF16),
-            pltpu.VMEM(scale.shape, F32),
-            pltpu.VMEM(fy.shape, BF16),
-            pltpu.VMEM(fz.shape, BF16),
+            pltpu.VMEM(forward.shape, BF16),
             pltpu.VMEM((8, 2 * length_z, 256), BF16),
             pltpu.VMEM((2 * channels * PITCH, length_z), F32),
-            pltpu.SemaphoreType.DMA((7,)),
+            pltpu.SemaphoreType.DMA((3,)),
         ],
         16, 10**9, 5 * 10**6,
-        *[in_hbm(one) for one in (field, cotangent, scale, fy, fz)],
-        in_specs=[hbm] * 5,
+        *[in_hbm(one) for one in (field, cotangent, forward)],
+        in_specs=[hbm] * 3,
     )
     spectra, spectral_weight, spread, gather = lax.optimization_barrier(
         (spectra, spectral_weight, spread_table(channels), gather_table(channels))

time: 37.4 us -> 37.2 us (level)
  no operation moved by 1% of the time
where the time goes in v5:
time: 37.2 us; the launch traced here: 36.9 us
  blocking collectives  17.2 us (46%)
  Pallas kernels  12.3 us (33%)
  starting transfers between devices  5.07 us (14%)
  waiting for transfers between devices  1.54 us (4%)
  between operations  0.72 us (2%)
    all_to_all x1, blocking collectives, on_device(): lax.all_to_all(spectra.reshape(groups, pairs, 128), 'gx', split_axis=0, c...  17.2 us
    pallas_call x5, Pallas kernels, call(): pl.pallas_call(kernel, out_shape=out_shape, **kwargs, scratch_shapes=scra...  12.3 us
    all_to_all x1, starting transfers between devices, on_device(): lax.all_to_all(grads.reshape(groups, count, 128), 'gx', split_axis=0, con...  3.51 us
    ppermute x1, starting transfers between devices, on_device(): other = lax.ppermute(other, 'dp', [(0, 1), (1, 0)])  1.55 us
    ppermute x1, waiting for transfers between devices, on_device(): other = lax.ppermute(other, 'dp', [(0, 1), (1, 0)])  1.16 us
  transfers between devices with their start and end apart: 2, of which 2 were waited for; matrix products, arithmetic and copies ran while one was open for 0% of the time, Pallas kernels for 13%

profile of v5, /device:TPU:0, one launch (start us, length us, event | category | flops | bytes accessed | tf_op | source)
XLA Modules:
  0.0 36.9 jit_solution(9330448969104052117)
XLA Ops:
  0.6 0.0 copy-start.2
  0.6 0.0 copy-start.5
  0.7 0.0 copy-start.6
  0.7 0.0 copy-start.7
  0.7 2.9 %shard_map.131 = f32[512,128]{1,0:T(8,128)S(1)} custom-call(bf16[32,128,128]{2,1,0:T(8,128)(2,1)} %bitcast.11, bf16[32,128,128]{2,1,0:T(8,128)(2,1)} %bitcast.12, bf16[304,256]{1,0:T(8,128)(2,1)} %constant.14.clone.table_hbm), custom_call_target="tpu_custom_call" | custom-call | flops 1000000000 | bytes 5000000 | tf_op jit(solution)/shard_map/pallas_call | solution.py:466
  3.6 17.2 %all_to_all.10 = f32[16,32,128]{2,1,0:T(8,128)S(1)} all-to-all(f32[16,32,128]{2,1,0:T(8,128)S(1)} %bitcast.9), channel_id=1, replica_groups=mesh['dp'=2,'gx'=16] {'gx'}, dimensions={0} | all-to-all | bytes 524288 | tf_op jit(solution)/shard_map/all_to_all | solution.py:522
  20.8 0.0 copy-start.3
  20.8 0.0 copy-start.4
  20.8 0.0 copy-done.2
  20.8 0.0 copy-done.5
  20.8 0.0 copy-done.6
  20.8 0.0 copy-done.7
  20.8 2.9 %shard_map.132 = (f32[32,8,128]{2,1,0:T(8,128)S(1)}, f32[32,8,128]{2,1,0:T(8,128)S(1)}, f32[256,128]{1,0:T(8,128)}) custom-call(f32[512,128]{1,0:T(8,128)S(1)} %bitcast.8, bf16[32,16,2048]{2,1,0:T(8,128)(2,1)S(1)} %copy-done.2, bf16[16,96]{1,0:T(8,128)(2,1)S(1)} %copy-done.7, bf16[16,96]{1,0:T(8,128)(2,1)S(1)} %copy-done.7, bf16[256,256]{1,0:T(8,128)(2,1)S(1)} %copy-done.6, ...), custom_call_target="tpu_custom_call" | custom-call | flops 1000000000 | bytes 4000000 | tf_op jit(solution)/shard_map/pallas_call | solution.py:466
  23.7 3.5 %all-to-all-start.1 = ((f32[16,16,128]{2,1,0:T(8,128)}), f32[16,16,128]{2,1,0:T(8,128)S(1)}, u32[]{:S(2)}, u32[]{:S(2)}) async-start(f32[16,16,128]{2,1,0:T(8,128)} %bitcast.4), calls=%async_computation.1 | async-start | bytes 262144 | tf_op jit(solution)/shard_map/all_to_all | solution.py:539
  27.3 1.6 %collective-permute-start = (f32[32,8,128]{2,1,0:T(8,128)S(1)}, f32[32,8,128]{2,1,0:T(8,128)S(1)}, u32[]{:S(2)}, u32[]{:S(2)}) collective-permute-start(f32[32,8,128]{2,1,0:T(8,128)S(1)} %get-tuple-element.20), channel_id=1, source_target_pairs={{0,16},{16,0},{1,17},{17,1},{2,18},{18,2},{3,19},{19,3},{4,20},{20... | collective-permute-start | bytes 393224 | tf_op jit(solution)/shard_map/ppermute | solution.py:559
  28.8 0.0 copy-done.3
  28.8 0.0 copy-done.4
  28.8 3.0 %shard_map.133 = (f32[32,128,128]{2,1,0:T(8,128)S(1)}, f32[32,8,2048]{2,1,0:T(8,128)S(1)}) custom-call(bf16[32,128,128]{2,1,0:T(8,128)(2,1)} %bitcast.13, bf16[32,32]{1,0:T(8,128)(2,1)S(1)} %copy-done.3, f32[32,8,128]{2,1,0:T(8,128)S(1)} %get-tuple-element.18.refs_2_, bf16[128,2304]{1,0:T(8,128)(2,1)S(1)} %copy-done.4), custom_call_target="tpu_custom_call" | custom-call | flops 4000000000 | bytes 5000000 | tf_op jit(solution)/shard_map/pallas_call | solution.py:466
  31.8 1.2 %collective-permute-done.modes_ref = f32[32,8,128]{2,1,0:T(8,128)S(1)} collective-permute-done((f32[32,8,128]{2,1,0:T(8,128)S(1)}, f32[32,8,128]{2,1,0:T(8,128)S(1)}, u32[]{:S(2)}, u32[]{:S(2)}) %collective-permute-start) | collective-permute-done | bytes 131104 | tf_op jit(solution)/shard_map/ppermute | solution.py:559
  33.0 0.0 copy-start
  33.0 0.0 copy-start.1
  33.0 1.8 %shard_map.135 = f32[32,8,2048]{2,1,0:T(8,128)} custom-call(f32[32,8,128]{2,1,0:T(8,128)S(1)} %collective-permute-done.modes_ref, bf16[128,2304]{1,0:T(8,128)(2,1)S(1)} %copy-done.4, f32[32,8,2048]{2,1,0:T(8,128)S(1)} %get-tuple-element.21.before_ref), custom_call_target="tpu_custom_call" | custom-call | flops 2000000000 | bytes 5000000 | tf_op jit(solution)/shard_map/pallas_call | solution.py:466
  34.8 0.4 %all-to-all-done.1 = f32[16,16,128]{2,1,0:T(8,128)S(1)} async-done(((f32[16,16,128]{2,1,0:T(8,128)}), f32[16,16,128]{2,1,0:T(8,128)S(1)}, u32[]{:S(2)}, u32[]{:S(2)}) %all-to-all-start.1) | async-done | bytes 131104 | tf_op jit(solution)/shard_map/all_to_all | solution.py:539
  35.2 0.0 copy-done
  35.2 0.0 copy-done.1
  35.2 1.8 %shard_map.134 = bf16[32,128,128]{2,1,0:T(8,128)(2,1)} custom-call(f32[256,128]{1,0:T(8,128)S(1)} %bitcast.7, f32[32,128,128]{2,1,0:T(8,128)S(1)} %get-tuple-element.19.linear_ref, bf16[2,2,256,256]{3,2,1,0:T(8,128)(2,1)S(1)} %copy-done, bf16[128,144]{1,0:T(8,128)(2,1)S(1)} %copy-done.1), custom_call_target="tpu_custom_call" | custom-call | flops 1000000000 | bytes 4000000 | tf_op jit(solution)/shard_map/pallas_call | solution.py:466
Async XLA Ops:
  0.6 20.2 %copy-start.2 = (bf16[32,16,2048]{2,1,0:T(8,128)(2,1)S(1)}, bf16[32,16,2048]{2,1,0:T(8,128)(2,1)}, u32[]{:S(2)}) copy-start(bf16[32,16,2048]{2,1,0:T(8,128)(2,1)} %weight_ref) | copy-start | bytes 6291460
  0.6 20.2 %copy-start.5 = (bf16[1024,256]{1,0:T(8,128)(2,1)S(1)}, bf16[1024,256]{1,0:T(8,128)(2,1)}, u32[]{:S(2)}) copy-start(bf16[1024,256]{1,0:T(8,128)(2,1)} %constant.16.clone.gather_ref) | copy-start | bytes 1572868
  0.7 20.2 %copy-start.6 = (bf16[256,256]{1,0:T(8,128)(2,1)S(1)}, bf16[256,256]{1,0:T(8,128)(2,1)}, u32[]{:S(2)}) copy-start(bf16[256,256]{1,0:T(8,128)(2,1)} %constant.15.clone.spread_ref) | copy-start | bytes 393220
  0.7 20.2 %copy-start.7 = (bf16[16,96]{1,0:T(8,128)(2,1)S(1)}, bf16[16,96]{1,0:T(8,128)(2,1)}, u32[]{:S(2)}) copy-start(bf16[16,96]{1,0:T(8,128)(2,1)} %constant.17.clone.fx_ref.ix_ref) | copy-start | bytes 9220
  20.8 8.0 %copy-start.3 = (bf16[32,32]{1,0:T(8,128)(2,1)S(1)}, bf16[32,32]{1,0:T(8,128)(2,1)}, u32[]{:S(2)}) copy-start(bf16[32,32]{1,0:T(8,128)(2,1)} %refs_1_.1) | copy-start | bytes 6148
  20.8 8.0 %copy-start.4 = (bf16[128,2304]{1,0:T(8,128)(2,1)S(1)}, bf16[128,2304]{1,0:T(8,128)(2,1)}, u32[]{:S(2)}) copy-start(bf16[128,2304]{1,0:T(8,128)(2,1)} %constant.18.clone.refs_3_.repeat_ref) | copy-start | bytes 1769476
  23.7 11.4 %all-to-all-start.1 = ((f32[16,16,128]{2,1,0:T(8,128)}), f32[16,16,128]{2,1,0:T(8,128)S(1)}, u32[]{:S(2)}, u32[]{:S(2)}) async-start(f32[16,16,128]{2,1,0:T(8,128)} %bitcast.4), calls=%async_computation.1 | async-start | bytes 262144 | tf_op jit(solution)/shard_map/all_to_all | solution.py:539
  27.3 5.7 %collective-permute-start = (f32[32,8,128]{2,1,0:T(8,128)S(1)}, f32[32,8,128]{2,1,0:T(8,128)S(1)}, u32[]{:S(2)}, u32[]{:S(2)}) collective-permute-start(f32[32,8,128]{2,1,0:T(8,128)S(1)} %get-tuple-element.20), channel_id=1, source_target_pairs={{0,16},{16,0},{1,17},{17,1},{2,18},{18,2},{3,19},{19,3},{4,20},{20... | collective-permute-start | bytes 393224 | tf_op jit(solution)/shard_map/ppermute | solution.py:559
  33.0 2.2 %copy-start = (bf16[2,2,256,256]{3,2,1,0:T(8,128)(2,1)S(1)}, bf16[2,2,256,256]{3,2,1,0:T(8,128)(2,1)}, u32[]{:S(2)}) copy-start(bf16[2,2,256,256]{3,2,1,0:T(8,128)(2,1)} %constant.19.clone.iz_ref) | copy-start | bytes 1572868
  33.0 2.2 %copy-start.1 = (bf16[128,144]{1,0:T(8,128)(2,1)S(1)}, bf16[128,144]{1,0:T(8,128)(2,1)}, u32[]{:S(2)}) copy-start(bf16[128,144]{1,0:T(8,128)(2,1)} %constant.20.clone.iy_ref) | copy-start | bytes 110596

commit v6 on v5

--- a/solution.py
+++ b/solution.py
@@ -138,8 +138,9 @@
         copies.append(copy)
         return copy
 
+    chunks = [start(field_hbm, data_ref.at[0])]
     table = start(table_hbm, table_ref)
-    chunks = [start(ref, data_ref.at[array]) for array, ref in enumerate((field_hbm, cot_hbm))]
+    chunks.append(start(cot_hbm, data_ref.at[1]))
     table.wait()
     along_y = jnp.concatenate([table_ref[:ROWS, :length_y], table_ref[:ROWS, length_y:]], axis=0)
     group = lax.broadcasted_iota(jnp.int32, (16, 256), 1) // M % 8

time: 37.2 us -> 37.2 us (level)
  no operation moved by 1% of the time
where the time goes in v6:
time: 37.2 us; the launch traced here: 36.9 us
  blocking collectives  17.2 us (46%)
  Pallas kernels  12.4 us (33%)
  starting transfers between devices  5.07 us (14%)
  waiting for transfers between devices  1.54 us (4%)
  between operations  0.72 us (2%)
    all_to_all x1, blocking collectives, on_device(): lax.all_to_all(spectra.reshape(groups, pairs, 128), 'gx', split_axis=0, c...  17.2 us
    pallas_call x5, Pallas kernels, call(): pl.pallas_call(kernel, out_shape=out_shape, **kwargs, scratch_shapes=scra...  12.4 us
    all_to_all x1, starting transfers between devices, on_device(): lax.all_to_all(grads.reshape(groups, count, 128), 'gx', split_axis=0, con...  3.51 us
    ppermute x1, starting transfers between devices, on_device(): other = lax.ppermute(other, 'dp', [(0, 1), (1, 0)])  1.55 us
    ppermute x1, waiting for transfers between devices, on_device(): other = lax.ppermute(other, 'dp', [(0, 1), (1, 0)])  1.16 us
  transfers between devices with their start and end apart: 2, of which 2 were waited for; matrix products, arithmetic and copies ran while one was open for 0% of the time, Pallas kernels for 13%

profile of v6, /device:TPU:0, one launch (start us, length us, event | category | flops | bytes accessed | tf_op | source)
XLA Modules:
  0.0 36.9 jit_solution(14465153625360294320)
XLA Ops:
  0.6 0.0 copy-start.2
  0.6 0.0 copy-start.5
  0.7 0.0 copy-start.6
  0.7 0.0 copy-start.7
  0.7 2.9 %shard_map.131 = f32[512,128]{1,0:T(8,128)S(1)} custom-call(bf16[32,128,128]{2,1,0:T(8,128)(2,1)} %bitcast.11, bf16[32,128,128]{2,1,0:T(8,128)(2,1)} %bitcast.12, bf16[304,256]{1,0:T(8,128)(2,1)} %constant.14.clone.table_hbm), custom_call_target="tpu_custom_call" | custom-call | flops 1000000000 | bytes 5000000 | tf_op jit(solution)/shard_map/pallas_call | solution.py:467
  3.6 17.2 %all_to_all.10 = f32[16,32,128]{2,1,0:T(8,128)S(1)} all-to-all(f32[16,32,128]{2,1,0:T(8,128)S(1)} %bitcast.9), channel_id=1, replica_groups=mesh['dp'=2,'gx'=16] {'gx'}, dimensions={0} | all-to-all | bytes 524288 | tf_op jit(solution)/shard_map/all_to_all | solution.py:523
  20.8 0.0 copy-start.3
  20.8 0.0 copy-start.4
  20.8 0.0 copy-done.2
  20.8 0.0 copy-done.5
  20.8 0.0 copy-done.6
  20.8 0.0 copy-done.7
  20.8 2.9 %shard_map.132 = (f32[32,8,128]{2,1,0:T(8,128)S(1)}, f32[32,8,128]{2,1,0:T(8,128)S(1)}, f32[256,128]{1,0:T(8,128)}) custom-call(f32[512,128]{1,0:T(8,128)S(1)} %bitcast.8, bf16[32,16,2048]{2,1,0:T(8,128)(2,1)S(1)} %copy-done.2, bf16[16,96]{1,0:T(8,128)(2,1)S(1)} %copy-done.7, bf16[16,96]{1,0:T(8,128)(2,1)S(1)} %copy-done.7, bf16[256,256]{1,0:T(8,128)(2,1)S(1)} %copy-done.6, ...), custom_call_target="tpu_custom_call" | custom-call | flops 1000000000 | bytes 4000000 | tf_op jit(solution)/shard_map/pallas_call | solution.py:467
  23.7 3.5 %all-to-all-start.1 = ((f32[16,16,128]{2,1,0:T(8,128)}), f32[16,16,128]{2,1,0:T(8,128)S(1)}, u32[]{:S(2)}, u32[]{:S(2)}) async-start(f32[16,16,128]{2,1,0:T(8,128)} %bitcast.4), calls=%async_computation.1 | async-start | bytes 262144 | tf_op jit(solution)/shard_map/all_to_all | solution.py:540
  27.3 1.6 %collective-permute-start = (f32[32,8,128]{2,1,0:T(8,128)S(1)}, f32[32,8,128]{2,1,0:T(8,128)S(1)}, u32[]{:S(2)}, u32[]{:S(2)}) collective-permute-start(f32[32,8,128]{2,1,0:T(8,128)S(1)} %get-tuple-element.20), channel_id=1, source_target_pairs={{0,16},{16,0},{1,17},{17,1},{2,18},{18,2},{3,19},{19,3},{4,20},{20... | collective-permute-start | bytes 393224 | tf_op jit(solution)/shard_map/ppermute | solution.py:560
  28.8 0.0 copy-done.3
  28.8 0.0 copy-done.4
  28.8 3.0 %shard_map.133 = (f32[32,128,128]{2,1,0:T(8,128)S(1)}, f32[32,8,2048]{2,1,0:T(8,128)S(1)}) custom-call(bf16[32,128,128]{2,1,0:T(8,128)(2,1)} %bitcast.13, bf16[32,32]{1,0:T(8,128)(2,1)S(1)} %copy-done.3, f32[32,8,128]{2,1,0:T(8,128)S(1)} %get-tuple-element.18.refs_2_, bf16[128,2304]{1,0:T(8,128)(2,1)S(1)} %copy-done.4), custom_call_target="tpu_custom_call" | custom-call | flops 4000000000 | bytes 5000000 | tf_op jit(solution)/shard_map/pallas_call | solution.py:467
  31.8 1.2 %collective-permute-done.modes_ref = f32[32,8,128]{2,1,0:T(8,128)S(1)} collective-permute-done((f32[32,8,128]{2,1,0:T(8,128)S(1)}, f32[32,8,128]{2,1,0:T(8,128)S(1)}, u32[]{:S(2)}, u32[]{:S(2)}) %collective-permute-start) | collective-permute-done | bytes 131104 | tf_op jit(solution)/shard_map/ppermute | solution.py:560
  33.0 0.0 copy-start
  33.0 0.0 copy-start.1
  33.0 1.8 %shard_map.135 = f32[32,8,2048]{2,1,0:T(8,128)} custom-call(f32[32,8,128]{2,1,0:T(8,128)S(1)} %collective-permute-done.modes_ref, bf16[128,2304]{1,0:T(8,128)(2,1)S(1)} %copy-done.4, f32[32,8,2048]{2,1,0:T(8,128)S(1)} %get-tuple-element.21.before_ref), custom_call_target="tpu_custom_call" | custom-call | flops 2000000000 | bytes 5000000 | tf_op jit(solution)/shard_map/pallas_call | solution.py:467
  34.8 0.4 %all-to-all-done.1 = f32[16,16,128]{2,1,0:T(8,128)S(1)} async-done(((f32[16,16,128]{2,1,0:T(8,128)}), f32[16,16,128]{2,1,0:T(8,128)S(1)}, u32[]{:S(2)}, u32[]{:S(2)}) %all-to-all-start.1) | async-done | bytes 131104 | tf_op jit(solution)/shard_map/all_to_all | solution.py:540
  35.2 0.0 copy-done
  35.2 0.0 copy-done.1
  35.2 1.8 %shard_map.134 = bf16[32,128,128]{2,1,0:T(8,128)(2,1)} custom-call(f32[256,128]{1,0:T(8,128)S(1)} %bitcast.7, f32[32,128,128]{2,1,0:T(8,128)S(1)} %get-tuple-element.19.linear_ref, bf16[2,2,256,256]{3,2,1,0:T(8,128)(2,1)S(1)} %copy-done, bf16[128,144]{1,0:T(8,128)(2,1)S(1)} %copy-done.1), custom_call_target="tpu_custom_call" | custom-call | flops 1000000000 | bytes 4000000 | tf_op jit(solution)/shard_map/pallas_call | solution.py:467
Async XLA Ops:
  0.6 20.2 %copy-start.2 = (bf16[32,16,2048]{2,1,0:T(8,128)(2,1)S(1)}, bf16[32,16,2048]{2,1,0:T(8,128)(2,1)}, u32[]{:S(2)}) copy-start(bf16[32,16,2048]{2,1,0:T(8,128)(2,1)} %weight_ref) | copy-start | bytes 6291460
  0.6 20.2 %copy-start.5 = (bf16[1024,256]{1,0:T(8,128)(2,1)S(1)}, bf16[1024,256]{1,0:T(8,128)(2,1)}, u32[]{:S(2)}) copy-start(bf16[1024,256]{1,0:T(8,128)(2,1)} %constant.16.clone.gather_ref) | copy-start | bytes 1572868
  0.7 20.2 %copy-start.6 = (bf16[256,256]{1,0:T(8,128)(2,1)S(1)}, bf16[256,256]{1,0:T(8,128)(2,1)}, u32[]{:S(2)}) copy-start(bf16[256,256]{1,0:T(8,128)(2,1)} %constant.15.clone.spread_ref) | copy-start | bytes 393220
  0.7 20.2 %copy-start.7 = (bf16[16,96]{1,0:T(8,128)(2,1)S(1)}, bf16[16,96]{1,0:T(8,128)(2,1)}, u32[]{:S(2)}) copy-start(bf16[16,96]{1,0:T(8,128)(2,1)} %constant.17.clone.fx_ref.ix_ref) | copy-start | bytes 9220
  20.8 8.0 %copy-start.3 = (bf16[32,32]{1,0:T(8,128)(2,1)S(1)}, bf16[32,32]{1,0:T(8,128)(2,1)}, u32[]{:S(2)}) copy-start(bf16[32,32]{1,0:T(8,128)(2,1)} %refs_1_.1) | copy-start | bytes 6148
  20.8 8.0 %copy-start.4 = (bf16[128,2304]{1,0:T(8,128)(2,1)S(1)}, bf16[128,2304]{1,0:T(8,128)(2,1)}, u32[]{:S(2)}) copy-start(bf16[128,2304]{1,0:T(8,128)(2,1)} %constant.18.clone.refs_3_.repeat_ref) | copy-start | bytes 1769476
  23.7 11.4 %all-to-all-start.1 = ((f32[16,16,128]{2,1,0:T(8,128)}), f32[16,16,128]{2,1,0:T(8,128)S(1)}, u32[]{:S(2)}, u32[]{:S(2)}) async-start(f32[16,16,128]{2,1,0:T(8,128)} %bitcast.4), calls=%async_computation.1 | async-start | bytes 262144 | tf_op jit(solution)/shard_map/all_to_all | solution.py:540
  27.3 5.7 %collective-permute-start = (f32[32,8,128]{2,1,0:T(8,128)S(1)}, f32[32,8,128]{2,1,0:T(8,128)S(1)}, u32[]{:S(2)}, u32[]{:S(2)}) collective-permute-start(f32[32,8,128]{2,1,0:T(8,128)S(1)} %get-tuple-element.20), channel_id=1, source_target_pairs={{0,16},{16,0},{1,17},{17,1},{2,18},{18,2},{3,19},{19,3},{4,20},{20... | collective-permute-start | bytes 393224 | tf_op jit(solution)/shard_map/ppermute | solution.py:560
  33.0 2.2 %copy-start = (bf16[2,2,256,256]{3,2,1,0:T(8,128)(2,1)S(1)}, bf16[2,2,256,256]{3,2,1,0:T(8,128)(2,1)}, u32[]{:S(2)}) copy-start(bf16[2,2,256,256]{3,2,1,0:T(8,128)(2,1)} %constant.19.clone.iz_ref) | copy-start | bytes 1572868
  33.0 2.2 %copy-start.1 = (bf16[128,144]{1,0:T(8,128)(2,1)S(1)}, bf16[128,144]{1,0:T(8,128)(2,1)}, u32[]{:S(2)}) copy-start(bf16[128,144]{1,0:T(8,128)(2,1)} %constant.20.clone.iy_ref) | copy-start | bytes 110596

commit v7 on v5

--- a/solution.py
+++ b/solution.py
@@ -90,24 +90,28 @@
 
 def spread_table(channels):
     copies = 128 // channels
-    table = np.zeros((2, 2, 2, channels, 2, copies, channels))
+    table = np.zeros((2, 2, 2, channels, 2, 2, copies, channels))
     eye = np.eye(channels)
     for part in range(2):
-        table[:, part, 1, :, part] = eye[:, None, :]
-    return table.reshape(8 * channels, 256).astype(ml_dtypes.bfloat16)
-
-
-LEVELS = 1
+        table[:, part, 1, :, 0, part] = eye[:, None, :]
+        table[:, part, 1, :, 1, part] = eye[:, None, np.arange(channels) ^ 16]
+    return table.reshape(8 * channels, 512).astype(ml_dtypes.bfloat16)
+
+
+def pair_table():
+    lane = np.arange(128)
+    first = (lane & 16) * 8
+    table = np.zeros((256, 256))
+    table[first + lane, lane] = 1.0
+    table[first + (lane ^ 16), 128 + lane] = 1.0
+    return table.astype(ml_dtypes.bfloat16)
 
 
 def gather_table(channels):
-    width = channels * channels >> LEVELS
+    width = channels * channels // 2
     place = np.arange(width)
-    block, lane = place // 128, place % 128
-    step = block << LEVELS
-    for level in range(LEVELS):
-        step = step + ((lane & 16 >> level) > 0) * (1 << level)
-    i = step * (128 // channels) + lane // channels
+    lane = place % 128
+    i = (place // 128 * 2 + (lane & 16) // 16) * (128 // channels) + lane // channels
     table = np.zeros((2, width, 2, 2, 2, channels))
     for part in range(2):
         table[part, place, 0, :, part, i] = 1.0
@@ -203,7 +207,7 @@
 
 
 def mid_kernel(
-    samples, planes_ref, weight_ref, fx_ref, ix_ref, spread_ref, gather_ref,
+    samples, planes_ref, weight_ref, fx_ref, ix_ref, spread_ref, pair_ref, gather_ref,
     mine_ref, other_ref, out_ref, rows_ref, split_ref,
 ):
     pairs, kept_x, _ = weight_ref.shape
@@ -234,44 +238,57 @@
                 other_ref[(ahead - 1) * pairs + q] = part
 
     square = weight_ref.shape[2] // 2
-    width = square >> LEVELS
-    lane = lax.broadcasted_iota(jnp.int32, (kept_x, 128), 1)
-
-    def merge(one, two, shift):
-        first = lane & shift == 0
-        moved = jnp.where(first, two, one)
-        moved = jnp.take_along_axis(moved, lane ^ shift, axis=1, mode="promise_in_bounds")
-        return jnp.where(first, one, two) + moved
-
-    def products(rows, q, start):
-        real, imag = rows[:, :128], rows[:, 128:]
-        w_real = weight_ref[q, :, start : start + 128].astype(F32)
-        w_imag = weight_ref[q, :, square + start : square + start + 128].astype(F32)
-        return real * w_real + imag * w_imag, imag * w_real - real * w_imag
-
+    width = square // 2
     grads = []
-    chunk = 8
+    chunk = min(pairs, 8)
     for first in range(0, pairs, chunk):
+        size = chunk * kept_x
+        base = 2 * first * kept_x
         high, low = split(rows_ref[first * kept_x : (first + chunk) * kept_x, :])
         spread = dot(jnp.concatenate([high, low], axis=1), spread_ref[...])
-        size = chunk * kept_x
-        base = 2 * first * kept_x
-        for place in range(chunk):
-            rows = spread[place * kept_x : (place + 1) * kept_x]
-            at = base + place * kept_x
-            for column in range(0, width, 128):
-                items = [
-                    products(rows, first + place, start)
-                    for start in range(column << LEVELS, column + 128 << LEVELS, 128)
-                ]
-                for part in range(2):
-                    values = [item[part] for item in items]
-                    for level in range(LEVELS):
-                        values = [merge(one, two, 16 >> level) for one, two in zip(values[::2], values[1::2])]
-                    high, low = split(values[0])
-                    at_column = part * width + column
-                    split_ref[at : at + kept_x, at_column : at_column + 128] = high
-                    split_ref[at + size : at + size + kept_x, at_column : at_column + 128] = low
+        real, imag, real_s, imag_s = (spread[:, 128 * k : 128 * k + 128] for k in range(4))
+
+        def paired(start):
+            block = weight_ref[first : first + chunk, :, start : start + 256].reshape(size, 256)
+            both = dot(block, pair_ref[...])
+            return both[:, :128], both[:, 128:]
+
+        lane = lax.broadcasted_iota(jnp.int32, (kept_x, 128), 1)
+        lower = lane & 16 == 0
+
+        def store(sums, at, column):
+            for part in range(2):
+                high, low = split(sums[part])
+                at_column = part * width + column
+                split_ref[base + at : base + at + kept_x, at_column : at_column + 128] = high
+                split_ref[base + size + at : base + size + at + kept_x, at_column : at_column + 128] = low
+
+        for column in range(0, width, 128):
+            by_dot = column // 128 % 4 == 3
+            if by_dot:
+                w_real, w_real_s = paired(2 * column)
+                w_imag, w_imag_s = paired(square + 2 * column)
+            for place in range(chunk):
+                rows = slice(place * kept_x, (place + 1) * kept_x)
+                r, i, rs, im_s = real[rows], imag[rows], real_s[rows], imag_s[rows]
+                if by_dot:
+                    wr, wi, wrs, wis = w_real[rows], w_imag[rows], w_real_s[rows], w_imag_s[rows]
+                    sums = (
+                        (r * wr + i * wi) + (rs * wrs + im_s * wis),
+                        (i * wr - r * wi) + (im_s * wrs - rs * wis),
+                    )
+                else:
+                    found = []
+                    for start in (2 * column, 2 * column + 128):
+                        wr = weight_ref[first + place, :, start : start + 128].astype(F32)
+                        wi = weight_ref[first + place, :, square + start : square + start + 128].astype(F32)
+                        found.append((r * wr + i * wi, i * wr - r * wi))
+                    sums = []
+                    for one, two in zip(*found):
+                        moved = jnp.where(lower, two, one)
+                        moved = jnp.take_along_axis(moved, lane ^ 16, axis=1, mode="promise_in_bounds")
+                        sums.append(jnp.where(lower, one, two) + moved)
+                store(sums, place * kept_x, column)
         both = dot(split_ref[base : base + 2 * size, :], gather_ref[...])
         grads.append(both[:size] + both[size:])
     grads = jnp.concatenate(grads, axis=0)
@@ -534,7 +551,7 @@
             pltpu.VMEM((2 * pairs * kept_x, gather.shape[0]), BF16),
         ],
         16, 10**9, 4 * 10**6,
-        received.reshape(width_x * pairs, 128), spectral_weight, fx, ix, spread, gather,
+        received.reshape(width_x * pairs, 128), spectral_weight, fx, ix, spread, pair_table(), gather,
     )
     returned = lax.all_to_all(
         grads.reshape(groups, count, 128), "gx", split_axis=0, concat_axis=0, tiled=True

time: 37.2 us -> 37.3 us (level)
  no operation moved by 1% of the time
where the time goes in v7:
time: 37.3 us; the launch traced here: 37 us
  blocking collectives  17.2 us (46%)
  Pallas kernels  12.4 us (33%)
  starting transfers between devices  5.07 us (14%)
  waiting for transfers between devices  1.53 us (4%)
  between operations  0.74 us (2%)
    all_to_all x1, blocking collectives, on_device(): lax.all_to_all(spectra.reshape(groups, pairs, 128), 'gx', split_axis=0, c...  17.2 us
    pallas_call x5, Pallas kernels, call(): pl.pallas_call(kernel, out_shape=out_shape, **kwargs, scratch_shapes=scra...  12.4 us
    all_to_all x1, starting transfers between devices, on_device(): lax.all_to_all(grads.reshape(groups, count, 128), 'gx', split_axis=0, con...  3.51 us
    ppermute x1, starting transfers between devices, on_device(): other = lax.ppermute(other, 'dp', [(0, 1), (1, 0)])  1.56 us
    ppermute x1, waiting for transfers between devices, on_device(): other = lax.ppermute(other, 'dp', [(0, 1), (1, 0)])  1.16 us
  transfers between devices with their start and end apart: 2, of which 2 were waited for; matrix products, arithmetic and copies ran while one was open for 0% of the time, Pallas kernels for 13%

profile of v7, /device:TPU:0, one launch (start us, length us, event | category | flops | bytes accessed | tf_op | source)
XLA Modules:
  0.0 37.0 jit_solution(3114774063010472680)
XLA Ops:
  0.6 0.0 copy-start.2
  0.6 0.0 copy-start.5
  0.7 0.0 copy-start.6
  0.7 0.0 copy-start.7
  0.7 0.0 copy-start.8
  0.7 2.9 %shard_map.140 = f32[512,128]{1,0:T(8,128)S(1)} custom-call(bf16[32,128,128]{2,1,0:T(8,128)(2,1)} %bitcast.11, bf16[32,128,128]{2,1,0:T(8,128)(2,1)} %bitcast.12, bf16[304,256]{1,0:T(8,128)(2,1)} %constant.16.clone.table_hbm), custom_call_target="tpu_custom_call" | custom-call | flops 1000000000 | bytes 5000000 | tf_op jit(solution)/shard_map/pallas_call | solution.py:483
  3.6 17.2 %all_to_all.10 = f32[16,32,128]{2,1,0:T(8,128)S(1)} all-to-all(f32[16,32,128]{2,1,0:T(8,128)S(1)} %bitcast.9), channel_id=1, replica_groups=mesh['dp'=2,'gx'=16] {'gx'}, dimensions={0} | all-to-all | bytes 524288 | tf_op jit(solution)/shard_map/all_to_all | solution.py:539
  20.8 0.0 copy-start.3
  20.8 0.0 copy-start.4
  20.8 0.0 copy-done.2
  20.8 0.0 copy-done.5
  20.8 0.0 copy-done.6
  20.8 0.0 copy-done.7
  20.9 0.0 copy-done.8
  20.9 3.0 %shard_map.141 = (f32[32,8,128]{2,1,0:T(8,128)S(1)}, f32[32,8,128]{2,1,0:T(8,128)S(1)}, f32[256,128]{1,0:T(8,128)}) custom-call(f32[512,128]{1,0:T(8,128)S(1)} %bitcast.8, bf16[32,16,2048]{2,1,0:T(8,128)(2,1)S(1)} %copy-done.2, bf16[16,96]{1,0:T(8,128)(2,1)S(1)} %copy-done.8, bf16[16,96]{1,0:T(8,128)(2,1)S(1)} %copy-done.8, bf16[256,512]{1,0:T(8,128)(2,1)S(1)} %copy-done.6, ...), custom_call_target="tpu_custom_call" | custom-call | flops 1000000000 | bytes 4000000 | tf_op jit(solution)/shard_map/pallas_call | solution.py:483
  23.8 3.5 %all-to-all-start.1 = ((f32[16,16,128]{2,1,0:T(8,128)}), f32[16,16,128]{2,1,0:T(8,128)S(1)}, u32[]{:S(2)}, u32[]{:S(2)}) async-start(f32[16,16,128]{2,1,0:T(8,128)} %bitcast.4), calls=%async_computation.1 | async-start | bytes 262144 | tf_op jit(solution)/shard_map/all_to_all | solution.py:556
  27.3 1.6 %collective-permute-start = (f32[32,8,128]{2,1,0:T(8,128)S(1)}, f32[32,8,128]{2,1,0:T(8,128)S(1)}, u32[]{:S(2)}, u32[]{:S(2)}) collective-permute-start(f32[32,8,128]{2,1,0:T(8,128)S(1)} %get-tuple-element.20), channel_id=1, source_target_pairs={{0,16},{16,0},{1,17},{17,1},{2,18},{18,2},{3,19},{19,3},{4,20},{20... | collective-permute-start | bytes 393224 | tf_op jit(solution)/shard_map/ppermute | solution.py:576
  28.9 0.0 copy-done.3
  28.9 0.0 copy-done.4
  28.9 3.0 %shard_map.142 = (f32[32,128,128]{2,1,0:T(8,128)S(1)}, f32[32,8,2048]{2,1,0:T(8,128)S(1)}) custom-call(bf16[32,128,128]{2,1,0:T(8,128)(2,1)} %bitcast.13, bf16[32,32]{1,0:T(8,128)(2,1)S(1)} %copy-done.3, f32[32,8,128]{2,1,0:T(8,128)S(1)} %get-tuple-element.18.refs_2_, bf16[128,2304]{1,0:T(8,128)(2,1)S(1)} %copy-done.4), custom_call_target="tpu_custom_call" | custom-call | flops 4000000000 | bytes 5000000 | tf_op jit(solution)/shard_map/pallas_call | solution.py:483
  31.9 1.2 %collective-permute-done.modes_ref = f32[32,8,128]{2,1,0:T(8,128)S(1)} collective-permute-done((f32[32,8,128]{2,1,0:T(8,128)S(1)}, f32[32,8,128]{2,1,0:T(8,128)S(1)}, u32[]{:S(2)}, u32[]{:S(2)}) %collective-permute-start) | collective-permute-done | bytes 131104 | tf_op jit(solution)/shard_map/ppermute | solution.py:576
  33.0 0.0 copy-start
  33.0 0.0 copy-start.1
  33.0 1.8 %shard_map.144 = f32[32,8,2048]{2,1,0:T(8,128)} custom-call(f32[32,8,128]{2,1,0:T(8,128)S(1)} %collective-permute-done.modes_ref, bf16[128,2304]{1,0:T(8,128)(2,1)S(1)} %copy-done.4, f32[32,8,2048]{2,1,0:T(8,128)S(1)} %get-tuple-element.21.before_ref), custom_call_target="tpu_custom_call" | custom-call | flops 2000000000 | bytes 5000000 | tf_op jit(solution)/shard_map/pallas_call | solution.py:483
  34.9 0.4 %all-to-all-done.1 = f32[16,16,128]{2,1,0:T(8,128)S(1)} async-done(((f32[16,16,128]{2,1,0:T(8,128)}), f32[16,16,128]{2,1,0:T(8,128)S(1)}, u32[]{:S(2)}, u32[]{:S(2)}) %all-to-all-start.1) | async-done | bytes 131104 | tf_op jit(solution)/shard_map/all_to_all | solution.py:556
  35.2 0.0 copy-done
  35.2 0.0 copy-done.1
  35.2 1.8 %shard_map.143 = bf16[32,128,128]{2,1,0:T(8,128)(2,1)} custom-call(f32[256,128]{1,0:T(8,128)S(1)} %bitcast.7, f32[32,128,128]{2,1,0:T(8,128)S(1)} %get-tuple-element.19.linear_ref, bf16[2,2,256,256]{3,2,1,0:T(8,128)(2,1)S(1)} %copy-done, bf16[128,144]{1,0:T(8,128)(2,1)S(1)} %copy-done.1), custom_call_target="tpu_custom_call" | custom-call | flops 1000000000 | bytes 4000000 | tf_op jit(solution)/shard_map/pallas_call | solution.py:483
Async XLA Ops:
  0.6 20.2 %copy-start.2 = (bf16[32,16,2048]{2,1,0:T(8,128)(2,1)S(1)}, bf16[32,16,2048]{2,1,0:T(8,128)(2,1)}, u32[]{:S(2)}) copy-start(bf16[32,16,2048]{2,1,0:T(8,128)(2,1)} %weight_ref) | copy-start | bytes 6291460
  0.6 20.2 %copy-start.5 = (bf16[1024,256]{1,0:T(8,128)(2,1)S(1)}, bf16[1024,256]{1,0:T(8,128)(2,1)}, u32[]{:S(2)}) copy-start(bf16[1024,256]{1,0:T(8,128)(2,1)} %constant.18.clone.gather_ref) | copy-start | bytes 1572868
  0.7 20.2 %copy-start.6 = (bf16[256,512]{1,0:T(8,128)(2,1)S(1)}, bf16[256,512]{1,0:T(8,128)(2,1)}, u32[]{:S(2)}) copy-start(bf16[256,512]{1,0:T(8,128)(2,1)} %constant.17.clone.spread_ref) | copy-start | bytes 786436
  0.7 20.2 %copy-start.7 = (bf16[256,256]{1,0:T(8,128)(2,1)S(1)}, bf16[256,256]{1,0:T(8,128)(2,1)}, u32[]{:S(2)}) copy-start(bf16[256,256]{1,0:T(8,128)(2,1)} %constant.20.clone.pair_ref) | copy-start | bytes 393220
  0.7 20.2 %copy-start.8 = (bf16[16,96]{1,0:T(8,128)(2,1)S(1)}, bf16[16,96]{1,0:T(8,128)(2,1)}, u32[]{:S(2)}) copy-start(bf16[16,96]{1,0:T(8,128)(2,1)} %constant.19.clone.fx_ref.ix_ref) | copy-start | bytes 9220
  20.8 8.1 %copy-start.3 = (bf16[32,32]{1,0:T(8,128)(2,1)S(1)}, bf16[32,32]{1,0:T(8,128)(2,1)}, u32[]{:S(2)}) copy-start(bf16[32,32]{1,0:T(8,128)(2,1)} %refs_1_.1) | copy-start | bytes 6148
  20.8 8.1 %copy-start.4 = (bf16[128,2304]{1,0:T(8,128)(2,1)S(1)}, bf16[128,2304]{1,0:T(8,128)(2,1)}, u32[]{:S(2)}) copy-start(bf16[128,2304]{1,0:T(8,128)(2,1)} %constant.21.clone.refs_3_.repeat_ref) | copy-start | bytes 1769476
  23.8 11.4 %all-to-all-start.1 = ((f32[16,16,128]{2,1,0:T(8,128)}), f32[16,16,128]{2,1,0:T(8,128)S(1)}, u32[]{:S(2)}, u32[]{:S(2)}) async-start(f32[16,16,128]{2,1,0:T(8,128)} %bitcast.4), calls=%async_computation.1 | async-start | bytes 262144 | tf_op jit(solution)/shard_map/all_to_all | solution.py:556
  27.3 5.7 %collective-permute-start = (f32[32,8,128]{2,1,0:T(8,128)S(1)}, f32[32,8,128]{2,1,0:T(8,128)S(1)}, u32[]{:S(2)}, u32[]{:S(2)}) collective-permute-start(f32[32,8,128]{2,1,0:T(8,128)S(1)} %get-tuple-element.20), channel_id=1, source_target_pairs={{0,16},{16,0},{1,17},{17,1},{2,18},{18,2},{3,19},{19,3},{4,20},{20... | collective-permute-start | bytes 393224 | tf_op jit(solution)/shard_map/ppermute | solution.py:576
  33.0 2.2 %copy-start = (bf16[2,2,256,256]{3,2,1,0:T(8,128)(2,1)S(1)}, bf16[2,2,256,256]{3,2,1,0:T(8,128)(2,1)}, u32[]{:S(2)}) copy-start(bf16[2,2,256,256]{3,2,1,0:T(8,128)(2,1)} %constant.22.clone.iz_ref) | copy-start | bytes 1572868
  33.0 2.2 %copy-start.1 = (bf16[128,144]{1,0:T(8,128)(2,1)S(1)}, bf16[128,144]{1,0:T(8,128)(2,1)}, u32[]{:S(2)}) copy-start(bf16[128,144]{1,0:T(8,128)(2,1)} %constant.23.clone.iy_ref) | copy-start | bytes 110596
